TPU v7x, 32 devices: a whole 2x2x4 slice. The times are simulated.
32 devices in a mesh: groups: 2 (over y), wide: 16 (over z, x, core), narrow: 1.
Axes of the slice: x: 2, y: 2, z: 4, core: 2. Of those that a mesh axis runs over, the one named last changes fastest.
Arguments:
- tokens: bfloat16 [4096, 8192], P(('groups', 'wide'), 'narrow'), parts along dimension 0, may hold values from -6 to 6
- adapter_down_weight: bfloat16 [16, 2, 4096, 128], P(None, 'narrow', 'wide'), may hold values from -0.0625 to 0.0625
- adapter_up_weight: bfloat16 [16, 2, 512, 128], P(None, 'narrow', 'wide'), may hold values from -0.75 to 0.75
- adapter_entry: int32 [16], replicated, may hold values from 0 to 15, each once
- adapter_of_request: int32 [8], P('groups'), parts along dimension 0, may hold values from 0 to 15
- token_blocks_per_request: int32 [8], P('groups'), parts along dimension 0, may hold values from 1 to 8, 16 in all
Outputs:
- key_delta: bfloat16 [4096, 1024], P(('groups', 'wide'), 'narrow'), parts along dimension 0
- value_delta: bfloat16 [4096, 1024], P(('groups', 'wide'), 'narrow'), parts along dimension 0
There are 2 independent parts, one for each index of `groups`. A program takes and returns all parts, laid end to end along the dimension named above; an argument that names none is the same for every part. Nothing has to cross between parts.
Inputs may be any that keep to these rules, and one draw needn't show every extreme that they name: `adapter_entry`: each table entry holds exactly one adapter. `token_blocks_per_request`: the counts sum to 16.
All inputs are finite; a program needn't handle non-finite values.
Results may differ from a plain program's by a relative error of at most 0.0049.
Values may be sent and summed in bfloat16 or wider, within the bound.
No kernel may reach another device: no remote copies, remote signals or barrier semaphores. Data moves between devices by JAX's collectives and lax.ppermute only.
A program may use at most 64 MiB of HBM per device.

v0:
```python
import jax
import jax.numpy as jnp
from jax import lax
from jax.sharding import PartitionSpec as P

BLK = 128


def block_tables(
    adapter_entry,
    adapter_of_request,
    token_blocks_per_request,
    block_count,
    request_count,
    adapter_count,
):
    request_ends = jnp.cumsum(token_blocks_per_request)
    block_index = jnp.arange(block_count, dtype=jnp.int32)
    request = jnp.sum((request_ends[None, :] <= block_index[:, None]).astype(jnp.int32), axis=1)
    pick_table = (request[:, None] == jnp.arange(request_count, dtype=jnp.int32)[None, :]).astype(
        jnp.int32
    )
    adapter = jnp.sum(pick_table * adapter_of_request[None, :], axis=1)
    slot_table = (adapter[:, None] == jnp.arange(adapter_count, dtype=jnp.int32)[None, :]).astype(
        jnp.int32
    )
    return jnp.sum(slot_table * adapter_entry[None, :], axis=1)


def body(
    tokens,
    adapter_down_weight,
    adapter_up_weight,
    adapter_entry,
    adapter_of_request,
    token_blocks_per_request,
):
    wide_count = lax.axis_size("wide")
    blocks_dev = tokens.shape[0] // BLK
    local_width = tokens.shape[1]
    paired_ranks = adapter_down_weight.shape[3]
    rank_count = paired_ranks // 2
    slot_ids = block_tables(
        adapter_entry,
        adapter_of_request,
        token_blocks_per_request,
        blocks_dev * wide_count,
        token_blocks_per_request.shape[0],
        adapter_entry.shape[0],
    )
    needed_adapters = slot_ids.reshape(wide_count, blocks_dev).T
    down_outgoing = adapter_down_weight[needed_adapters]
    up_outgoing = adapter_up_weight[needed_adapters]
    got_down, got_up = (
        lax.all_to_all(down_outgoing, "wide", split_axis=1, concat_axis=3, tiled=True),
        lax.all_to_all(up_outgoing, "wide", split_axis=1, concat_axis=3, tiled=True),
    )
    got_down = got_down.reshape(blocks_dev, local_width, paired_ranks)
    block_rows = tokens.reshape(blocks_dev, BLK, local_width)
    shrink = jnp.einsum("btd,bdr->btr", block_rows, got_down, preferred_element_type=jnp.float32)
    low_rank = lax.psum(shrink, "narrow").astype(jnp.bfloat16)
    got_up = got_up.reshape(blocks_dev, -1, paired_ranks)
    delta_key = jnp.einsum(
        "btr,bjr->btj",
        low_rank[..., :rank_count],
        got_up[..., :rank_count],
        preferred_element_type=jnp.float32,
    )
    delta_value = jnp.einsum(
        "btr,bjr->btj",
        low_rank[..., rank_count:],
        got_up[..., rank_count:],
        preferred_element_type=jnp.float32,
    )
    out_cols = got_up.shape[1]
    key_delta = delta_key.reshape(blocks_dev * BLK, out_cols).astype(jnp.bfloat16)
    value_delta = delta_value.reshape(blocks_dev * BLK, out_cols).astype(jnp.bfloat16)
    return (key_delta, value_delta)


def solution(mesh):
    return jax.shard_map(
        body,
        mesh=mesh,
        in_specs=(
            P(("groups", "wide"), "narrow"),
            P(None, "narrow", "wide", None),
            P(None, "narrow", "wide", None),
            P(),
            P("groups"),
            P("groups"),
        ),
        out_specs=(P(("groups", "wide"), "narrow"), P(("groups", "wide"), "narrow")),
        check_vma=False,
    )
```

profile of v0, /device:TPU:15, one launch (start us, length us, event | category | flops | bytes accessed | tf_op | source)
XLA Modules:
  0.0 78.9 jit_solution(2228068476304398935)
XLA Ops:
  0.6 0.0 copy-start
  0.6 1.0 %reduce-window.8 = s32[4,1]{0,1:T(1,128)S(1)} reduce-window(s32[4,1]{0,1:T(1,128)} %bitcast.44, s32[]{:T(128)} %constant.8.clone.1), window={size=4x1 pad=3_0x0_0}, to_apply=%region_0.0 | reduce-window | flops 12 | bytes 36 | tf_op jit(solution)/shard_map/reduce-window.3
  1.6 0.1 convert_reduce_fusion
  1.7 0.7 select_reduce_fusion.1
  2.4 0.8 %select_reduce_fusion = s32[16]{0:T(128)S(1)} fusion(s32[16]{0:T(128)} %param.9, s32[16]{0:T(128)S(1)} %select_reduce_fusion.1), kind=kLoop, calls=%fused_computation.10 | loop fusion | flops 752 | bytes 192 | tf_op jit(solution)/shard_map/reduce_sum | solution.py:27
  3.3 2.2 %gather_fusion.1 = bf16[16,2,32,128]{3,2,1,0:T(8,128)(2,1)} fusion(bf16[16,2,32,128]{3,2,1,0:T(8,128)(2,1)} %param.8, s32[1024]{0:T(1024)S(1)} %pad_clamp_fusion), kind=kCustom, calls=%fused_computation.1 | custom fusion | bytes 524352 | tf_op jit(solution)/shard_map/gather | solution.py:53
  5.5 6.6 %all-to-all-start.1 = ((bf16[1,16,2,32,128]{4,3,2,0,1:T(8,128)(2,1)}), bf16[1,16,2,32,128]{4,3,2,0,1:T(8,128)(2,1)S(1)}, u32[]{:S(2)}, u32[]{:S(2)}) async-start(bf16[1,16,2,32,128]{4,3,2,0,1:T(8,128)(2,1)} %bitcast.13), calls=%async_computation.1 | async-start | bytes 524288 | tf_op jit(solution)/shard_map/all_to_all | solution.py:56
  12.1 0.0 copy-done
  12.1 2.1 %gather_fusion = bf16[16,2,256,128]{3,2,1,0:T(8,128)(2,1)} fusion(bf16[16,2,256,128]{3,2,1,0:T(8,128)(2,1)S(1)} %copy-done, s32[1024]{0:T(1024)S(1)} %pad_clamp_fusion), kind=kCustom, calls=%fused_computation | custom fusion | bytes 4194368 | tf_op jit(solution)/shard_map/gather | solution.py:52
  14.2 5.8 %all-to-all-done.1 = bf16[1,16,2,32,128]{4,3,2,0,1:T(8,128)(2,1)S(1)} async-done(((bf16[1,16,2,32,128]{4,3,2,0,1:T(8,128)(2,1)}), bf16[1,16,2,32,128]{4,3,2,0,1:T(8,128)(2,1)S(1)}, u32[]{:S(2)}, u32[]{:S(2)}) %all-to-all-start.1) | async-done | bytes 262176 | tf_op jit(solution)/shard_map/all_to_all | solution.py:56
  20.0 6.4 %all-to-all-start = ((bf16[1,16,2,256,128]{4,3,2,0,1:T(8,128)(2,1)}), bf16[1,16,2,256,128]{4,3,2,0,1:T(8,128)(2,1)}, u32[]{:S(2)}, u32[]{:S(2)}) async-start(bf16[1,16,2,256,128]{4,3,2,0,1:T(8,128)(2,1)} %bitcast.40), calls=%async_computation | async-start | bytes 4194304 | tf_op jit(solution)/shard_map/all_to_all | solution.py:55
  26.4 47.5 %all-to-all-done = bf16[1,16,2,256,128]{4,3,2,0,1:T(8,128)(2,1)} async-done(((bf16[1,16,2,256,128]{4,3,2,0,1:T(8,128)(2,1)}), bf16[1,16,2,256,128]{4,3,2,0,1:T(8,128)(2,1)}, u32[]{:S(2)}, u32[]{:S(2)}) %all-to-all-start) | async-done | bytes 2097184 | tf_op jit(solution)/shard_map/all_to_all | solution.py:55
  74.0 0.0 copy-start.1
  74.0 1.9 %copy.15 = bf16[1,16,2,256,128]{4,3,1,2,0:T(8,128)(2,1)S(1)} copy(bf16[1,16,2,256,128]{4,3,2,0,1:T(8,128)(2,1)} %all-to-all-done) | data formatting | bytes 4194304 | tf_op jit(solution)/shard_map/all_to_all | solution.py:55
  75.9 0.3 copy-done.1
  76.2 0.7 fusion
  76.9 1.0 %convolution_convert_fusion = bf16[128,1024]{1,0:T(8,128)(2,1)} fusion(bf16[1,1024,128]{2,1,0:T(8,128)(2,1)S(1)} %bitcast.42, bf16[1,128,128]{1,2,0:T(8,128)(2,1)S(1)} %fusion), kind=kOutput, calls=%fused_computation.2 | convolution fusion | flops 16908288 | bytes 540672 | tf_op jit(solution)/shard_map/btr,bjr->btj/dot_general | solution.py:69
  78.0 1.0 %convolution_convert_fusion.1 = bf16[128,1024]{1,0:T(8,128)(2,1)} fusion(bf16[1,1024,128]{2,1,0:T(8,128)(2,1)S(1)} %bitcast.43, bf16[1,128,128]{1,2,0:T(8,128)(2,1)S(1)} %fusion), kind=kOutput, calls=%fused_computation.3 | convolution fusion | flops 16908288 | bytes 540672 | tf_op jit(solution)/shard_map/btr,bjr->btj/dot_general | solution.py:63
  (3 shorter events, 0.0 us)
Async XLA Ops:
  0.6 11.5 %copy-start = (bf16[16,2,256,128]{3,2,1,0:T(8,128)(2,1)S(1)}, bf16[16,2,256,128]{3,2,1,0:T(8,128)(2,1)}, u32[]{:S(2)}) copy-start(bf16[16,2,256,128]{3,2,1,0:T(8,128)(2,1)} %param.7) | copy-start | bytes 6291460
  5.5 14.5 %all-to-all-start.1 = ((bf16[1,16,2,32,128]{4,3,2,0,1:T(8,128)(2,1)}), bf16[1,16,2,32,128]{4,3,2,0,1:T(8,128)(2,1)S(1)}, u32[]{:S(2)}, u32[]{:S(2)}) async-start(bf16[1,16,2,32,128]{4,3,2,0,1:T(8,128)(2,1)} %bitcast.13), calls=%async_computation.1 | async-start | bytes 524288 | tf_op jit(solution)/shard_map/all_to_all | solution.py:56
  20.0 53.9 %all-to-all-start = ((bf16[1,16,2,256,128]{4,3,2,0,1:T(8,128)(2,1)}), bf16[1,16,2,256,128]{4,3,2,0,1:T(8,128)(2,1)}, u32[]{:S(2)}, u32[]{:S(2)}) async-start(bf16[1,16,2,256,128]{4,3,2,0,1:T(8,128)(2,1)} %bitcast.40), calls=%async_computation | async-start | bytes 4194304 | tf_op jit(solution)/shard_map/all_to_all | solution.py:55
  74.0 2.2 %copy-start.1 = (bf16[128,8192]{1,0:T(8,128)(2,1)S(1)}, bf16[128,8192]{1,0:T(8,128)(2,1)}, u32[]{:S(2)}) copy-start(bf16[128,8192]{1,0:T(8,128)(2,1)} %param.6) | copy-start | bytes 6291460
where the time goes:
time: 79.3 us; the launch traced here: 78.9 us
  waiting for transfers between devices  53.4 us (67%)
  starting transfers between devices  12.9 us (16%)
  local copies, waits for them, and re-layouts  6.58 us (8%)
  matrix products  2.74 us (3%)
  other arithmetic  2.65 us (3%)
    all_to_all x1, waiting for transfers between devices, body(): lax.all_to_all(down_outgoing, 'wide', split_axis=1, concat_axis=3, tiled=...  47.5 us
    all_to_all x1, starting transfers between devices, body(): lax.all_to_all(up_outgoing, 'wide', split_axis=1, concat_axis=3, tiled=True)  6.55 us
    all_to_all x1, starting transfers between devices, body(): lax.all_to_all(down_outgoing, 'wide', split_axis=1, concat_axis=3, tiled=...  6.38 us
    all_to_all x1, waiting for transfers between devices, body(): lax.all_to_all(up_outgoing, 'wide', split_axis=1, concat_axis=3, tiled=True)  5.84 us
    gather x1, local copies, waits for them, and re-layouts, body(): up_outgoing = adapter_up_weight[needed_adapters]  2.23 us
    gather x1, local copies, waits for them, and re-layouts, body(): down_outgoing = adapter_down_weight[needed_adapters]  2.11 us
    all_to_all x1, local copies, waits for them, and re-layouts, body(): lax.all_to_all(down_outgoing, 'wide', split_axis=1, concat_axis=3, tiled=...  1.88 us
  transfers between devices with their start and end apart: 2, of which 2 were waited for; matrix products, arithmetic and copies ran while one was open for 3% of the time, Pallas kernels for 0%

commit v1 on v0

--- a/solution.py
+++ b/solution.py
@@ -1,9 +1,13 @@
 import jax
 import jax.numpy as jnp
 from jax import lax
+from jax.experimental import pallas as pl
+from jax.experimental.pallas import tpu as pltpu
 from jax.sharding import PartitionSpec as P
 
 BLK = 128
+PLANE = 4
+SLOTS = 3
 
 
 def block_tables(
@@ -27,7 +31,7 @@
     return jnp.sum(slot_table * adapter_entry[None, :], axis=1)
 
 
-def body(
+def direct_body(
     tokens,
     adapter_down_weight,
     adapter_up_weight,
@@ -78,9 +82,302 @@
     return (key_delta, value_delta)
 
 
+def swap(value, step):
+    count = lax.axis_size("wide")
+    return lax.ppermute(value, "wide", [(i, i ^ step) for i in range(count)])
+
+
+def pick(index, values):
+    got = values[0]
+    for i in range(1, len(values)):
+        got = jnp.where(index == i, values[i], got)
+    return got
+
+
+def prepare_kernel(
+    planes,
+    entry_ref,
+    adapter_ref,
+    counts_ref,
+    tokens_ref,
+    down_ref,
+    up_ref,
+    table_ref,
+    *refs,
+):
+    others = planes - 1
+    factors_out = refs[:others]
+    tokens_out = refs[others : others + PLANE - 1]
+    tokens_sem, down_sem, up_sem = refs[others + PLANE - 1 :]
+    me = lax.axis_index("wide")
+    column, plane = lax.rem(me, PLANE), lax.div(me, PLANE)
+    run, up_run = down_ref.shape[2], up_ref.shape[2]
+    copies = []
+    for k in range(1, PLANE):
+        for piece in range(2 * planes):
+            start = piece * PLANE * run + (column ^ k) * run
+            copies.append(
+                pltpu.make_async_copy(
+                    tokens_ref.at[:, pl.ds(pl.multiple_of(start, run), run)],
+                    tokens_out[k - 1].at[piece],
+                    tokens_sem.at[k - 1, piece],
+                )
+            )
+            copies[-1].start()
+
+    requests = counts_ref.shape[0]
+    ends, total = [], 0
+    for q in range(requests):
+        total = total + counts_ref[q]
+        ends.append(total)
+    entries = [entry_ref[adapter_ref[q]] for q in range(requests)]
+    slots, places, most = [], [], jnp.int32(1)
+    for p in range(planes):
+        ids = []
+        for i in range(PLANE):
+            got = entries[0]
+            for q in range(1, requests):
+                got = jnp.where(ends[q - 1] <= p * PLANE + i, entries[q], got)
+            ids.append(got)
+        place, held, count = [jnp.int32(0)], [ids[0]] * SLOTS, jnp.int32(1)
+        for i in range(1, PLANE):
+            found = count
+            for j in range(i):
+                found = jnp.where(ids[i] == ids[j], place[j], found)
+            place.append(found)
+            held = [jnp.where(found == s, ids[i], held[s]) for s in range(SLOTS)]
+            count = jnp.maximum(count, found + 1)
+        slots.append(held)
+        places.append(place)
+        most = jnp.maximum(most, count)
+    for k in range(1, planes):
+        there = plane ^ k
+        for s in range(SLOTS):
+            slot = pick(there, [slots[p][s] for p in range(planes)])
+            copies.append(
+                pltpu.make_async_copy(
+                    down_ref.at[slot],
+                    factors_out[k - 1].at[s, :, pl.ds(0, run)],
+                    down_sem.at[k - 1, s],
+                )
+            )
+            copies[-1].start()
+            copies.append(
+                pltpu.make_async_copy(
+                    up_ref.at[slot],
+                    factors_out[k - 1].at[s, :, pl.ds(run, up_run)],
+                    up_sem.at[k - 1, s],
+                )
+            )
+            copies[-1].start()
+    here = [pick(plane, [places[p][i] for p in range(planes)]) for i in range(PLANE)]
+    for k in range(PLANE):
+        table_ref[k] = pick(column ^ k, here)
+    for s in range(SLOTS):
+        table_ref[PLANE + s] = pick(plane, [slots[p][s] for p in range(planes)])
+    table_ref[PLANE + SLOTS] = most
+    for copy in copies:
+        copy.wait()
+
+
+def prepare(planes, tokens, down, up, entry, adapter, counts):
+    run, ranks = down.shape[2:]
+    hbm = pl.BlockSpec(memory_space=pl.ANY)
+    smem = pl.BlockSpec(memory_space=pltpu.SMEM)
+    others = planes - 1
+    factors = jax.ShapeDtypeStruct((SLOTS, 2, run + up.shape[2], ranks), down.dtype)
+    return pl.pallas_call(
+        lambda *refs: prepare_kernel(planes, *refs),
+        out_shape=[jax.ShapeDtypeStruct((PLANE + SLOTS + 1,), jnp.int32)]
+        + [factors] * others
+        + [jax.ShapeDtypeStruct((2 * planes, BLK, run), tokens.dtype)] * (PLANE - 1),
+        in_specs=[smem] * 3 + [hbm] * 3,
+        out_specs=[smem] + [hbm] * (others + PLANE - 1),
+        scratch_shapes=[
+            pltpu.SemaphoreType.DMA((PLANE - 1, 2 * planes)),
+            pltpu.SemaphoreType.DMA((others, SLOTS)),
+            pltpu.SemaphoreType.DMA((others, SLOTS)),
+        ],
+        compiler_params=pltpu.CompilerParams(vmem_limit_bytes=2**20),
+        name="prepare",
+    )(entry, adapter, counts, tokens, down, up)
+
+
+def shrink_kernel(planes, table_ref, tokens_ref, down_ref, up_ref, *refs):
+    others = planes - 1
+    got_tokens = refs[: PLANE - 1]
+    got_factors = refs[PLANE - 1 : PLANE - 1 + others]
+    own_ref, *sends, ups = refs[PLANE - 1 + others : 2 * PLANE + others]
+    rows, factors, rows_sem, factors_sem, up_sem = refs[2 * PLANE + others :]
+    me = lax.axis_index("wide")
+    column, plane = lax.rem(me, PLANE), lax.div(me, PLANE)
+    run, up_run = down_ref.shape[2], up_ref.shape[2]
+    slots = factors.shape[0]
+    copies = []
+    for piece in range(2 * planes):
+        start = piece * PLANE * run + column * run
+        copies.append(
+            pltpu.make_async_copy(
+                tokens_ref.at[:, pl.ds(pl.multiple_of(start, run), run)],
+                rows.at[0, piece],
+                rows_sem.at[0, piece],
+            )
+        )
+    for k in range(1, PLANE):
+        copies.append(pltpu.make_async_copy(got_tokens[k - 1], rows.at[k], rows_sem.at[k, 0]))
+    for s in range(slots):
+        slot = table_ref[PLANE + s]
+        copies.append(
+            pltpu.make_async_copy(
+                down_ref.at[slot], factors.at[s, plane, :, pl.ds(0, run)], factors_sem.at[0, s]
+            )
+        )
+        copies.append(
+            pltpu.make_async_copy(
+                up_ref.at[slot], factors.at[s, plane, :, pl.ds(run, up_run)], up_sem.at[s]
+            )
+        )
+        for d in range(1, planes):
+            copies.append(
+                pltpu.make_async_copy(
+                    got_factors[d - 1].at[s], factors.at[s, plane ^ d], factors_sem.at[d, s]
+                )
+            )
+    for copy in copies:
+        copy.start()
+    for copy in copies:
+        copy.wait()
+    for k in range(PLANE):
+        place = table_ref[k]
+        total = jnp.zeros(own_ref.shape, jnp.float32)
+        for half in range(2):
+            for p in range(planes):
+                total += jnp.dot(
+                    rows[k, half * planes + p],
+                    factors[place, p, half, pl.ds(0, run)],
+                    preferred_element_type=jnp.float32,
+                )
+        up_rows = factors[place, :, :, pl.ds(run, up_run)]
+        if k == 0:
+            own_ref[...] = total
+            ups[...] = up_rows
+        else:
+            sends[k - 1][pl.ds(0, BLK)] = total.astype(sends[k - 1].dtype)
+            sends[k - 1][pl.ds(BLK, 2 * planes * up_run)] = up_rows.reshape(-1, up_rows.shape[-1])
+
+
+def shrink(planes, slots, table, tokens, down, up, got_tokens, got_factors):
+    hbm = pl.BlockSpec(memory_space=pl.ANY)
+    vmem = pl.BlockSpec(memory_space=pltpu.VMEM)
+    run, ranks = down.shape[2:]
+    up_run = up.shape[2]
+    send = jax.ShapeDtypeStruct((BLK + 2 * planes * up_run, ranks), tokens.dtype)
+    return pl.pallas_call(
+        lambda *refs: shrink_kernel(planes, *refs),
+        out_shape=[jax.ShapeDtypeStruct((BLK, ranks), jnp.float32)] + [send] * (PLANE - 1)
+        + [jax.ShapeDtypeStruct((planes, 2, up_run, ranks), up.dtype)],
+        in_specs=[pl.BlockSpec(memory_space=pltpu.SMEM)] + [hbm] * (planes + PLANE + 1),
+        out_specs=[vmem] * (PLANE + 1),
+        scratch_shapes=[
+            pltpu.VMEM((PLANE, 2 * planes, BLK, run), tokens.dtype),
+            pltpu.VMEM((slots, planes, 2, run + up_run, ranks), down.dtype),
+            pltpu.SemaphoreType.DMA((PLANE, 2 * planes)),
+            pltpu.SemaphoreType.DMA((planes, slots)),
+            pltpu.SemaphoreType.DMA((slots,)),
+        ],
+        compiler_params=pltpu.CompilerParams(vmem_limit_bytes=8 * 2**20),
+        name="shrink",
+    )(table, tokens, down, up, *got_tokens, *got_factors)
+
+
+def expand_kernel(own_ref, up_ref, *refs):
+    got = refs[: PLANE - 1]
+    key_ref, value_ref, factor = refs[PLANE - 1 :]
+    column = lax.rem(lax.axis_index("wide"), PLANE)
+    planes, _, up_run, ranks = up_ref.shape
+    total = own_ref[...]
+    factor[:, :, column] = up_ref[...]
+    for k in range(1, PLANE):
+        total += got[k - 1][pl.ds(0, BLK)].astype(jnp.float32)
+        factor[:, :, column ^ k] = got[k - 1][pl.ds(BLK, 2 * planes * up_run)].reshape(up_ref.shape)
+    low_rank = total.astype(jnp.bfloat16)
+    is_key = lax.broadcasted_iota(jnp.int32, low_rank.shape, 1) < ranks // 2
+    zero = jnp.zeros_like(low_rank)
+    both = jnp.concatenate(
+        [jnp.where(is_key, low_rank, zero), jnp.where(is_key, zero, low_rank)], axis=0
+    )
+    for half in range(2):
+        for p in range(planes):
+            delta = lax.dot_general(
+                both,
+                factor[p, half].reshape(PLANE * up_run, ranks),
+                (((1,), (1,)), ((), ())),
+                preferred_element_type=jnp.float32,
+            ).astype(jnp.bfloat16)
+            columns = pl.ds((half * planes + p) * PLANE * up_run, PLANE * up_run)
+            key_ref[:, columns] = delta[:BLK]
+            value_ref[:, columns] = delta[BLK:]
+
+
+def expand(own, up, got):
+    planes, _, up_run, ranks = up.shape
+    columns = 2 * planes * PLANE * up_run
+    vmem = pl.BlockSpec(memory_space=pltpu.VMEM)
+    return pl.pallas_call(
+        expand_kernel,
+        out_shape=[jax.ShapeDtypeStruct((BLK, columns), jnp.bfloat16)] * 2,
+        in_specs=[vmem] * (PLANE + 1),
+        out_specs=[vmem] * 2,
+        scratch_shapes=[pltpu.VMEM((planes, 2, PLANE, up_run, ranks), jnp.bfloat16)],
+        compiler_params=pltpu.CompilerParams(vmem_limit_bytes=4 * 2**20),
+        name="expand",
+    )(own, up, *got)
+
+
+def plane_body(
+    tokens,
+    adapter_down_weight,
+    adapter_up_weight,
+    adapter_entry,
+    adapter_of_request,
+    token_blocks_per_request,
+):
+    planes = lax.axis_size("wide") // PLANE
+    others = planes - 1
+    table, *sends = prepare(
+        planes,
+        tokens,
+        adapter_down_weight,
+        adapter_up_weight,
+        adapter_entry,
+        adapter_of_request,
+        token_blocks_per_request,
+    )
+
+    def rest(slots, table, tokens, down, up, factors_sends, tokens_sends):
+        got_factors = [swap(factors_sends[d - 1][:slots], d * PLANE) for d in range(1, planes)]
+        got_tokens = [swap(tokens_sends[k - 1], k) for k in range(1, PLANE)]
+        own, *sends, ups = shrink(planes, slots, table, tokens, down, up, got_tokens, got_factors)
+        got = [swap(sends[k - 1], k) for k in range(1, PLANE)]
+        return tuple(expand(own, ups, got))
+
+    return lax.cond(
+        table[PLANE + SLOTS] > 2,
+        lambda *operands: rest(3, *operands),
+        lambda *operands: rest(2, *operands),
+        table,
+        tokens,
+        adapter_down_weight,
+        adapter_up_weight,
+        sends[:others],
+        sends[others:],
+    )
+
+
 def solution(mesh):
+    by_plane = mesh.shape["wide"] == 16 and mesh.shape["narrow"] == 1
     return jax.shard_map(
-        body,
+        plane_body if by_plane else direct_body,
         mesh=mesh,
         in_specs=(
             P(("groups", "wide"), "narrow"),

time: 79.3 us -> 55.5 us (0.70)
  the two profiles are of different devices: /device:TPU:15 before, /device:TPU:0 now
where the time goes in v1:
time: 55.5 us; the launch traced here: 55.3 us
  waiting for transfers between devices  21.9 us (39%)
  starting transfers between devices  21.4 us (39%)
  Pallas kernels  8.02 us (14%)
  local copies, waits for them, and re-layouts  2.61 us (5%)
  between operations  1.33 us (2%)
    ppermute x9, waiting for transfers between devices, swap(): return lax.ppermute(value, 'wide', [(i, i ^ step) for i in range(count)])  21.9 us
    ppermute x9, starting transfers between devices, swap(): return lax.ppermute(value, 'wide', [(i, i ^ step) for i in range(count)])  21.4 us
    pallas_call x1, Pallas kernels, prepare(): pl.pallas_call(lambda *refs: prepare_kernel(planes, *refs), out_shape=[ja...  3.7 us
    pallas_call x1, Pallas kernels, shrink(): pl.pallas_call(lambda *refs: shrink_kernel(planes, *refs), out_shape=[jax...  3.22 us
    unnamed x12, local copies, waits for them, and re-layouts  1.97 us
  transfers between devices with their start and end apart: 9, of which 5 were waited for; matrix products, arithmetic and copies ran while one was open for 0% of the time, Pallas kernels for 0%

profile of v1, /device:TPU:0, one launch (start us, length us, event | category | flops | bytes accessed | tf_op | source)
XLA Modules:
  0.0 55.3 jit_solution(2118726401881301524)
XLA Ops:
  0.6 0.0 copy-start
  0.6 0.6 %copy-done = s32[16]{0:T(128)S(1)} copy-done((s32[16]{0:T(128)S(1)}, s32[16]{0:T(128)}, u32[]{:S(2)}) %copy-start) | copy-done | bytes 88
  1.3 0.0 copy-start.1
  1.3 0.7 %copy-done.1 = s32[4]{0:T(128)S(1)} copy-done((s32[4]{0:T(128)S(1)}, s32[4]{0:T(128)}, u32[]{:S(2)}) %copy-start.1) | copy-done | bytes 40
  1.9 0.0 copy-start.2
  1.9 0.7 %copy-done.2 = s32[4]{0:T(128)S(1)} copy-done((s32[4]{0:T(128)S(1)}, s32[4]{0:T(128)}, u32[]{:S(2)}) %copy-start.2) | copy-done | bytes 40
  2.6 0.0 copy-start.3
  2.6 0.0 copy-start.4
  2.6 0.0 copy-start.5
  2.6 3.7 %prepare.1 = (s32[8]{0:T(128)S(1)}, bf16[3,2,288,128]{3,2,1,0:T(8,128)(2,1)S(1)}, bf16[3,2,288,128]{3,2,1,0:T(8,128)(2,1)S(1)}, bf16[3,2,288,128]{3,2,1,0:T(8,12...) custom-call(s32[16]{0:T(128)S(1)} %copy-done, ...), custom_call_target="tpu_custom_call" | custom-call | tf_op jit(solution)/shard_map/prepare/pallas_call | solution.py:189
  6.3 0.6 %slice.12 = s32[1]{0:T(128)} slice(s32[8]{0:T(128)S(1)} %get-tuple-element.79), slice={[7:8]} | slice | bytes 8 | tf_op jit(solution)/shard_map/slice | solution.py:365
  7.5 0.0 copy-done.3
  7.6 0.0 copy-done.4
  7.6 0.0 copy-done.5
  7.6 47.7 %conditional.1 = ((bf16[128,1024]{1,0:T(8,128)(2,1)}, bf16[128,1024]{1,0:T(8,128)(2,1)})) conditional(s32[]{:T(128)} %bitcast, (bf16[8,128,256]{2,1,0:T(8,128)(2,1)S(1)}, bf16[8,128,256]{2,1,0:T(8,128)(2,1)S(1)}, bf16[8,128,256]{2,1,0:T(8,128)(2,1)S(1)}, bf16[3,2,288,128]{3,2,1,0:T(8,128)(2,1)S(1)}, bf16[3,2,288,128]{3,2,1,0:T(8,128)(2,1)S(1)}, ...), branch_computations={%region_0.0_spmd, %region_1.0_spmd} | conditional | bytes 12779888 | solution.py:364
  7.6 5.1 %collective-permute-start.5 = (bf16[2,2,288,128]{3,2,1,0:T(8,128)(2,1)S(1)}, bf16[2,2,288,128]{3,2,1,0:T(8,128)(2,1)S(1)}, u32[]{:S(2)}, u32[]{:S(2)}) collective-permute-start(bf16[2,2,288,128]{3,2,1,0:T(8,128)(2,1)S(1)} %slice.10), channel_id=1, source_target_pairs={{0,12},{1,13},{2,14},{3,15},{4,8},{5,9},{6,10},{7,11},{8,4},{9,5},... | collective-permute-start | bytes 884744 | tf_op jit(solution)/shard_map/cond/branch_0_fun/ppermute | solution.py:87
  12.7 0.0 collective-permute-start
  12.7 1.5 %collective-permute-start.1 = (bf16[8,128,256]{2,1,0:T(8,128)(2,1)S(1)}, bf16[8,128,256]{2,1,0:T(8,128)(2,1)S(1)}, u32[]{:S(2)}, u32[]{:S(2)}) collective-permute-start(bf16[8,128,256]{2,1,0:T(8,128)(2,1)S(1)} %get-tuple-element.45), channel_id=1, source_target_pairs={{0,2},{1,3},{2,0},{3,1},{4,6},{5,7},{6,4},{7,5},{8,10},{9,11},{10,... | collective-permute-start | bytes 1572872 | tf_op jit(solution)/shard_map/cond/branch_0_fun/ppermute | solution.py:87
  14.2 0.4 collective-permute-start.2
  14.6 0.1 collective-permute-start.4
  14.7 5.9 %collective-permute-done.5.refs_9_ = bf16[2,2,288,128]{3,2,1,0:T(8,128)(2,1)S(1)} collective-permute-done((bf16[2,2,288,128]{3,2,1,0:T(8,128)(2,1)S(1)}, bf16[2,2,288,128]{3,2,1,0:T(8,128)(2,1)S(1)}, u32[]{:S(2)}, u32[]{:S(2)}) %collective-permute-start.5) | collective-permute-done | bytes 294944 | tf_op jit(solution)/shard_map/cond/branch_0_fun/ppermute | solution.py:87
  20.7 12.4 %collective-permute-start.3 = (bf16[2,2,288,128]{3,2,1,0:T(8,128)(2,1)S(1)}, bf16[2,2,288,128]{3,2,1,0:T(8,128)(2,1)S(1)}, u32[]{:S(2)}, u32[]{:S(2)}) collective-permute-start(bf16[2,2,288,128]{3,2,1,0:T(8,128)(2,1)S(1)} %slice.8), channel_id=1, source_target_pairs={{0,4},{1,5},{2,6},{3,7},{4,0},{5,1},{6,2},{7,3},{8,12},{9,13},{10,... | collective-permute-start | bytes 884744 | tf_op jit(solution)/shard_map/cond/branch_0_fun/ppermute | solution.py:87
  33.1 4.9 %collective-permute-done.4.refs_8_ = bf16[2,2,288,128]{3,2,1,0:T(8,128)(2,1)S(1)} collective-permute-done((bf16[2,2,288,128]{3,2,1,0:T(8,128)(2,1)S(1)}, bf16[2,2,288,128]{3,2,1,0:T(8,128)(2,1)S(1)}, u32[]{:S(2)}, u32[]{:S(2)}) %collective-permute-start.4) | collective-permute-done | bytes 294944 | tf_op jit(solution)/shard_map/cond/branch_0_fun/ppermute | solution.py:87
  38.0 6.0 %collective-permute-done.3.refs_7_ = bf16[2,2,288,128]{3,2,1,0:T(8,128)(2,1)S(1)} collective-permute-done((bf16[2,2,288,128]{3,2,1,0:T(8,128)(2,1)S(1)}, bf16[2,2,288,128]{3,2,1,0:T(8,128)(2,1)S(1)}, u32[]{:S(2)}, u32[]{:S(2)}) %collective-permute-start.3) | collective-permute-done | bytes 294944 | tf_op jit(solution)/shard_map/cond/branch_0_fun/ppermute | solution.py:87
  44.0 0.0 collective-permute-done.refs_4_
  44.0 0.0 collective-permute-done.1.refs_5_
  44.0 0.0 collective-permute-done.2.refs_6_
  44.0 3.2 %shrink.2 = (f32[128,128]{1,0:T(8,128)S(1)}, bf16[384,128]{1,0:T(8,128)(2,1)S(1)}, bf16[384,128]{1,0:T(8,128)(2,1)S(1)}, bf16[384,128]{1,0:T(8,128)(2,1)S(1)}, bf16[4,2,32,128]{3,2,1,0:T(8,128)(2,1)S(1)}) custom-call(s32[8]{0:T(128)S(1)} %get-tuple-element.40.refs_0_, bf16[128,8192]{1,0:T(8,128)(2,1)S(1)} %get-tuple-element.41.refs_1_, ...), custom_call_target="tpu_custom_call" | custom-call | tf_op jit(solution)/shard_map/cond/branch_0_fun/shrink/pallas_call | solution.py:275
  47.2 0.1 collective-permute-start.6
  47.3 1.6 %collective-permute-start.7 = (bf16[384,128]{1,0:T(8,128)(2,1)S(1)}, bf16[384,128]{1,0:T(8,128)(2,1)S(1)}, u32[]{:S(2)}, u32[]{:S(2)}) collective-permute-start(bf16[384,128]{1,0:T(8,128)(2,1)S(1)} %get-tuple-element.53), channel_id=1, source_target_pairs={{0,2},{1,3},{2,0},{3,1},{4,6},{5,7},{6,4},{7,5},{8,10},{9,11},{10,... | collective-permute-start | bytes 294920 | tf_op jit(solution)/shard_map/cond/branch_0_fun/ppermute | solution.py:87
  48.8 0.3 collective-permute-start.8
  49.2 0.0 collective-permute-done.6.refs_0_
  49.2 3.8 %collective-permute-done.7.refs_1_ = bf16[384,128]{1,0:T(8,128)(2,1)S(1)} collective-permute-done((bf16[384,128]{1,0:T(8,128)(2,1)S(1)}, bf16[384,128]{1,0:T(8,128)(2,1)S(1)}, u32[]{:S(2)}, u32[]{:S(2)}) %collective-permute-start.7) | collective-permute-done | bytes 98336 | tf_op jit(solution)/shard_map/cond/branch_0_fun/ppermute | solution.py:87
  53.0 1.2 %collective-permute-done.8.refs_2_ = bf16[384,128]{1,0:T(8,128)(2,1)S(1)} collective-permute-done((bf16[384,128]{1,0:T(8,128)(2,1)S(1)}, bf16[384,128]{1,0:T(8,128)(2,1)S(1)}, u32[]{:S(2)}, u32[]{:S(2)}) %collective-permute-start.8) | collective-permute-done | bytes 98336 | tf_op jit(solution)/shard_map/cond/branch_0_fun/ppermute | solution.py:87
  54.2 1.1 %expand.2 = (bf16[128,1024]{1,0:T(8,128)(2,1)}, bf16[128,1024]{1,0:T(8,128)(2,1)}) custom-call(f32[128,128]{1,0:T(8,128)S(1)} %get-tuple-element.50.own_ref, bf16[4,2,32,128]{3,2,1,0:T(8,128)(2,1)S(1)} %get-tuple-element.51.up_ref, bf16[384,128]{1,0:T(8,128)(2,1)S(1)} %collective-permute-done.6.refs_0_, bf16[384,128]{1,0:T(8,128)(2,1)S(1)} %collective-permute-done.7.refs_1_, ...), custom_call_target="tpu_custom_call" | custom-call | tf_op jit(solution)/shard_map/cond/branch_0_fun/expand/pallas_call | solution.py:326
  (3 shorter events, 0.1 us)
Async XLA Ops:
  0.6 0.7 %copy-start = (s32[16]{0:T(128)S(1)}, s32[16]{0:T(128)}, u32[]{:S(2)}) copy-start(s32[16]{0:T(128)} %refs_0_.1) | copy-start | bytes 196
  1.3 0.7 %copy-start.1 = (s32[4]{0:T(128)S(1)}, s32[4]{0:T(128)}, u32[]{:S(2)}) copy-start(s32[4]{0:T(128)} %refs_1_.1) | copy-start | bytes 52
  1.9 0.7 %copy-start.2 = (s32[4]{0:T(128)S(1)}, s32[4]{0:T(128)}, u32[]{:S(2)}) copy-start(s32[4]{0:T(128)} %refs_2_.1) | copy-start | bytes 52
  2.6 5.0 %copy-start.3 = (bf16[128,8192]{1,0:T(8,128)(2,1)S(1)}, bf16[128,8192]{1,0:T(8,128)(2,1)}, u32[]{:S(2)}) copy-start(bf16[128,8192]{1,0:T(8,128)(2,1)} %refs_3_.1) | copy-start | bytes 6291460
  2.6 5.0 %copy-start.4 = (bf16[16,2,256,128]{3,2,1,0:T(8,128)(2,1)S(1)}, bf16[16,2,256,128]{3,2,1,0:T(8,128)(2,1)}, u32[]{:S(2)}) copy-start(bf16[16,2,256,128]{3,2,1,0:T(8,128)(2,1)} %refs_4_.1) | copy-start | bytes 6291460
  2.6 5.0 %copy-start.5 = (bf16[16,2,32,128]{3,2,1,0:T(8,128)(2,1)S(1)}, bf16[16,2,32,128]{3,2,1,0:T(8,128)(2,1)}, u32[]{:S(2)}) copy-start(bf16[16,2,32,128]{3,2,1,0:T(8,128)(2,1)} %refs_5_.1) | copy-start | bytes 786436
  7.6 13.1 %collective-permute-start.5 = (bf16[2,2,288,128]{3,2,1,0:T(8,128)(2,1)S(1)}, bf16[2,2,288,128]{3,2,1,0:T(8,128)(2,1)S(1)}, u32[]{:S(2)}, u32[]{:S(2)}) collective-permute-start(bf16[2,2,288,128]{3,2,1,0:T(8,128)(2,1)S(1)} %slice.10), channel_id=1, source_target_pairs={{0,12},{1,13},{2,14},{3,15},{4,8},{5,9},{6,10},{7,11},{8,4},{9,5},... | collective-permute-start | bytes 884744 | tf_op jit(solution)/shard_map/cond/branch_0_fun/ppermute | solution.py:87
  12.7 31.2 %collective-permute-start = (bf16[8,128,256]{2,1,0:T(8,128)(2,1)S(1)}, bf16[8,128,256]{2,1,0:T(8,128)(2,1)S(1)}, u32[]{:S(2)}, u32[]{:S(2)}) collective-permute-start(bf16[8,128,256]{2,1,0:T(8,128)(2,1)S(1)} %get-tuple-element.44), channel_id=1, source_target_pairs={{0,1},{1,0},{2,3},{3,2},{4,5},{5,4},{6,7},{7,6},{8,9},{9,8},{10,11... | collective-permute-start | bytes 1572872 | tf_op jit(solution)/shard_map/cond/branch_0_fun/ppermute | solution.py:87
  12.7 31.2 %collective-permute-start.1 = (bf16[8,128,256]{2,1,0:T(8,128)(2,1)S(1)}, bf16[8,128,256]{2,1,0:T(8,128)(2,1)S(1)}, u32[]{:S(2)}, u32[]{:S(2)}) collective-permute-start(bf16[8,128,256]{2,1,0:T(8,128)(2,1)S(1)} %get-tuple-element.45), channel_id=1, source_target_pairs={{0,2},{1,3},{2,0},{3,1},{4,6},{5,7},{6,4},{7,5},{8,10},{9,11},{10,... | collective-permute-start | bytes 1572872 | tf_op jit(solution)/shard_map/cond/branch_0_fun/ppermute | solution.py:87
  14.2 29.8 %collective-permute-start.2 = (bf16[8,128,256]{2,1,0:T(8,128)(2,1)S(1)}, bf16[8,128,256]{2,1,0:T(8,128)(2,1)S(1)}, u32[]{:S(2)}, u32[]{:S(2)}) collective-permute-start(bf16[8,128,256]{2,1,0:T(8,128)(2,1)S(1)} %get-tuple-element.46), channel_id=1, source_target_pairs={{0,3},{1,2},{2,1},{3,0},{4,7},{5,6},{6,5},{7,4},{8,11},{9,10},{10,... | collective-permute-start | bytes 1572872 | tf_op jit(solution)/shard_map/cond/branch_0_fun/ppermute | solution.py:87
  14.6 23.3 %collective-permute-start.4 = (bf16[2,2,288,128]{3,2,1,0:T(8,128)(2,1)S(1)}, bf16[2,2,288,128]{3,2,1,0:T(8,128)(2,1)S(1)}, u32[]{:S(2)}, u32[]{:S(2)}) collective-permute-start(bf16[2,2,288,128]{3,2,1,0:T(8,128)(2,1)S(1)} %slice.9), channel_id=1, source_target_pairs={{0,8},{1,9},{2,10},{3,11},{4,12},{5,13},{6,14},{7,15},{8,0},{9,1},... | collective-permute-start | bytes 884744 | tf_op jit(solution)/shard_map/cond/branch_0_fun/ppermute | solution.py:87
  20.7 23.3 %collective-permute-start.3 = (bf16[2,2,288,128]{3,2,1,0:T(8,128)(2,1)S(1)}, bf16[2,2,288,128]{3,2,1,0:T(8,128)(2,1)S(1)}, u32[]{:S(2)}, u32[]{:S(2)}) collective-permute-start(bf16[2,2,288,128]{3,2,1,0:T(8,128)(2,1)S(1)} %slice.8), channel_id=1, source_target_pairs={{0,4},{1,5},{2,6},{3,7},{4,0},{5,1},{6,2},{7,3},{8,12},{9,13},{10,... | collective-permute-start | bytes 884744 | tf_op jit(solution)/shard_map/cond/branch_0_fun/ppermute | solution.py:87
  47.2 1.9 %collective-permute-start.6 = (bf16[384,128]{1,0:T(8,128)(2,1)S(1)}, bf16[384,128]{1,0:T(8,128)(2,1)S(1)}, u32[]{:S(2)}, u32[]{:S(2)}) collective-permute-start(bf16[384,128]{1,0:T(8,128)(2,1)S(1)} %get-tuple-element.52), channel_id=1, source_target_pairs={{0,1},{1,0},{2,3},{3,2},{4,5},{5,4},{6,7},{7,6},{8,9},{9,8},{10,11... | collective-permute-start | bytes 294920 | tf_op jit(solution)/shard_map/cond/branch_0_fun/ppermute | solution.py:87
  47.3 5.7 %collective-permute-start.7 = (bf16[384,128]{1,0:T(8,128)(2,1)S(1)}, bf16[384,128]{1,0:T(8,128)(2,1)S(1)}, u32[]{:S(2)}, u32[]{:S(2)}) collective-permute-start(bf16[384,128]{1,0:T(8,128)(2,1)S(1)} %get-tuple-element.53), channel_id=1, source_target_pairs={{0,2},{1,3},{2,0},{3,1},{4,6},{5,7},{6,4},{7,5},{8,10},{9,11},{10,... | collective-permute-start | bytes 294920 | tf_op jit(solution)/shard_map/cond/branch_0_fun/ppermute | solution.py:87
  48.8 5.3 %collective-permute-start.8 = (bf16[384,128]{1,0:T(8,128)(2,1)S(1)}, bf16[384,128]{1,0:T(8,128)(2,1)S(1)}, u32[]{:S(2)}, u32[]{:S(2)}) collective-permute-start(bf16[384,128]{1,0:T(8,128)(2,1)S(1)} %get-tuple-element.54), channel_id=1, source_target_pairs={{0,3},{1,2},{2,1},{3,0},{4,7},{5,6},{6,5},{7,4},{8,11},{9,10},{10,... | collective-permute-start | bytes 294920 | tf_op jit(solution)/shard_map/cond/branch_0_fun/ppermute | solution.py:87

commit v2 on v1

v2 whole, which is shorter than its diff:
```python
import jax
import jax.numpy as jnp
from jax import lax
from jax.experimental import pallas as pl
from jax.experimental.pallas import tpu as pltpu
from jax.sharding import PartitionSpec as P

BLK = 128
PLANE = 4
SLOTS = 3
USUAL = 2


def block_tables(
    adapter_entry,
    adapter_of_request,
    token_blocks_per_request,
    block_count,
    request_count,
    adapter_count,
):
    request_ends = jnp.cumsum(token_blocks_per_request)
    block_index = jnp.arange(block_count, dtype=jnp.int32)
    request = jnp.sum((request_ends[None, :] <= block_index[:, None]).astype(jnp.int32), axis=1)
    pick_table = (request[:, None] == jnp.arange(request_count, dtype=jnp.int32)[None, :]).astype(
        jnp.int32
    )
    adapter = jnp.sum(pick_table * adapter_of_request[None, :], axis=1)
    slot_table = (adapter[:, None] == jnp.arange(adapter_count, dtype=jnp.int32)[None, :]).astype(
        jnp.int32
    )
    return jnp.sum(slot_table * adapter_entry[None, :], axis=1)


def direct_body(
    tokens,
    adapter_down_weight,
    adapter_up_weight,
    adapter_entry,
    adapter_of_request,
    token_blocks_per_request,
):
    wide_count = lax.axis_size("wide")
    blocks_dev = tokens.shape[0] // BLK
    local_width = tokens.shape[1]
    paired_ranks = adapter_down_weight.shape[3]
    rank_count = paired_ranks // 2
    slot_ids = block_tables(
        adapter_entry,
        adapter_of_request,
        token_blocks_per_request,
        blocks_dev * wide_count,
        token_blocks_per_request.shape[0],
        adapter_entry.shape[0],
    )
    needed_adapters = slot_ids.reshape(wide_count, blocks_dev).T
    down_outgoing = adapter_down_weight[needed_adapters]
    up_outgoing = adapter_up_weight[needed_adapters]
    got_down, got_up = (
        lax.all_to_all(down_outgoing, "wide", split_axis=1, concat_axis=3, tiled=True),
        lax.all_to_all(up_outgoing, "wide", split_axis=1, concat_axis=3, tiled=True),
    )
    got_down = got_down.reshape(blocks_dev, local_width, paired_ranks)
    block_rows = tokens.reshape(blocks_dev, BLK, local_width)
    shrink = jnp.einsum("btd,bdr->btr", block_rows, got_down, preferred_element_type=jnp.float32)
    low_rank = lax.psum(shrink, "narrow").astype(jnp.bfloat16)
    got_up = got_up.reshape(blocks_dev, -1, paired_ranks)
    delta_key = jnp.einsum(
        "btr,bjr->btj",
        low_rank[..., :rank_count],
        got_up[..., :rank_count],
        preferred_element_type=jnp.float32,
    )
    delta_value = jnp.einsum(
        "btr,bjr->btj",
        low_rank[..., rank_count:],
        got_up[..., rank_count:],
        preferred_element_type=jnp.float32,
    )
    out_cols = got_up.shape[1]
    key_delta = delta_key.reshape(blocks_dev * BLK, out_cols).astype(jnp.bfloat16)
    value_delta = delta_value.reshape(blocks_dev * BLK, out_cols).astype(jnp.bfloat16)
    return (key_delta, value_delta)


def swap(value, step):
    count = lax.axis_size("wide")
    return lax.ppermute(value, "wide", [(i, i ^ step) for i in range(count)])


def pick(index, values):
    got = values[0]
    for i in range(1, len(values)):
        got = jnp.where(index == i, values[i], got)
    return got


def prepare_kernel(
    planes,
    entry_hbm,
    adapter_hbm,
    counts_hbm,
    tokens_ref,
    down_ref,
    up_ref,
    places_ref,
    many_ref,
    *refs,
):
    factors_out = refs[:planes]
    tokens_out = refs[planes : planes + PLANE]
    entry_ref, adapter_ref, counts_ref = refs[planes + PLANE : planes + PLANE + 3]
    small_sem, tokens_sem, down_sem, up_sem = refs[planes + PLANE + 3 :]
    me = lax.axis_index("wide")
    column, plane = lax.rem(me, PLANE), lax.div(me, PLANE)
    run, up_run = down_ref.shape[2], up_ref.shape[2]
    small = [
        pltpu.make_async_copy(entry_hbm, entry_ref, small_sem.at[0]),
        pltpu.make_async_copy(adapter_hbm, adapter_ref, small_sem.at[1]),
        pltpu.make_async_copy(counts_hbm, counts_ref, small_sem.at[2]),
    ]
    for copy in small:
        copy.start()
    copies = []
    for k in range(PLANE):
        for piece in range(2 * planes):
            start = piece * PLANE * run + (column ^ k) * run
            copies.append(
                pltpu.make_async_copy(
                    tokens_ref.at[:, pl.ds(pl.multiple_of(start, run), run)],
                    tokens_out[k].at[piece],
                    tokens_sem.at[k, piece],
                )
            )
            copies[-1].start()
    for copy in small:
        copy.wait()

    requests = counts_ref.shape[0]
    ends, total = [], 0
    for q in range(requests):
        total = total + counts_ref[q]
        ends.append(total)
    entries = [entry_ref[adapter_ref[q]] for q in range(requests)]
    slots, places, most = [], [], jnp.int32(1)
    for p in range(planes):
        ids = []
        for i in range(PLANE):
            got = entries[0]
            for q in range(1, requests):
                got = jnp.where(ends[q - 1] <= p * PLANE + i, entries[q], got)
            ids.append(got)
        place, held, count = [jnp.int32(0)], [ids[0]] * SLOTS, jnp.int32(1)
        for i in range(1, PLANE):
            found = count
            for j in range(i):
                found = jnp.where(ids[i] == ids[j], place[j], found)
            place.append(found)
            held = [jnp.where(found == s, ids[i], held[s]) for s in range(SLOTS)]
            count = jnp.maximum(count, found + 1)
        slots.append(held)
        places.append(place)
        most = jnp.maximum(most, count)

    def send_rows(k, s):
        slot = pick(plane ^ k, [held[s] for held in slots])
        out = factors_out[k].at[s]
        return (
            pltpu.make_async_copy(down_ref.at[slot], out.at[:, pl.ds(0, run)], down_sem.at[k, s]),
            pltpu.make_async_copy(up_ref.at[slot], out.at[:, pl.ds(run, up_run)], up_sem.at[k, s]),
        )

    for k in range(planes):
        for s in range(USUAL):
            for copy in send_rows(k, s):
                copy.start()
                copies.append(copy)
    here = [pick(plane, [place[i] for place in places]) for i in range(PLANE)]
    for k in range(PLANE):
        places_ref[k] = pick(column ^ k, here)
    many_ref[0] = jnp.where(most > USUAL, 1, 0)

    @pl.when(most > USUAL)
    def _():
        more = [copy for k in range(planes) for s in range(USUAL, SLOTS) for copy in send_rows(k, s)]
        for copy in more:
            copy.start()
        for copy in more:
            copy.wait()

    for copy in copies:
        copy.wait()


def prepare(planes, tokens, down, up, entry, adapter, counts):
    run, ranks = down.shape[2:]
    hbm = pl.BlockSpec(memory_space=pltpu.HBM)
    smem = pl.BlockSpec(memory_space=pltpu.SMEM)
    factors = jax.ShapeDtypeStruct((SLOTS, 2, run + up.shape[2], ranks), down.dtype)
    rows = jax.ShapeDtypeStruct((2 * planes, BLK, run), tokens.dtype)
    return pl.pallas_call(
        lambda *refs: prepare_kernel(planes, *refs),
        out_shape=[jax.ShapeDtypeStruct((PLANE,), jnp.int32), jax.ShapeDtypeStruct((1,), jnp.int32)]
        + [factors] * planes
        + [rows] * PLANE,
        in_specs=[hbm] * 6,
        out_specs=[smem] * 2 + [pl.BlockSpec(memory_space=pltpu.VMEM)] * (planes + PLANE),
        scratch_shapes=[
            pltpu.SMEM(entry.shape, jnp.int32),
            pltpu.SMEM(adapter.shape, jnp.int32),
            pltpu.SMEM(counts.shape, jnp.int32),
            pltpu.SemaphoreType.DMA((3,)),
            pltpu.SemaphoreType.DMA((PLANE, 2 * planes)),
            pltpu.SemaphoreType.DMA((planes, SLOTS)),
            pltpu.SemaphoreType.DMA((planes, SLOTS)),
        ],
        compiler_params=pltpu.CompilerParams(vmem_limit_bytes=59 * 2**20),
        name="prepare",
    )(entry, adapter, counts, tokens, down, up)


def shrink_kernel(planes, slots, run, places_ref, *refs):
    rows = refs[:PLANE]
    factors = refs[PLANE : PLANE + planes]
    own_ref, *sends, ups = refs[PLANE + planes :]
    plane = lax.div(lax.axis_index("wide"), PLANE)
    up_run, ranks = ups.shape[2:]
    places = [places_ref[k] for k in range(PLANE)]
    for k in range(PLANE):
        for d in range(planes):
            for half in range(2):
                up_rows = factors[d][places[k], half, pl.ds(run, up_run)]
                if k == 0:
                    ups[plane ^ d, half] = up_rows
                else:
                    start = BLK + ((plane ^ d) * 2 + half) * up_run
                    sends[k - 1][pl.ds(pl.multiple_of(start, up_run), up_run)] = up_rows
    total = jnp.zeros((PLANE * BLK, slots * ranks), jnp.float32)
    for d in range(planes):
        for half in range(2):
            total += jnp.dot(
                jnp.concatenate([rows[k][half * planes + (plane ^ d)] for k in range(PLANE)], axis=0),
                jnp.concatenate([factors[d][s, half, pl.ds(0, run)] for s in range(slots)], axis=1),
                preferred_element_type=jnp.float32,
            )
    for k in range(PLANE):
        of_block = total[k * BLK : (k + 1) * BLK]
        mine = pick(places[k], [of_block[:, s * ranks : (s + 1) * ranks] for s in range(slots)])
        if k == 0:
            own_ref[...] = mine
        else:
            sends[k - 1][pl.ds(0, BLK)] = mine.astype(sends[k - 1].dtype)


def shrink(planes, slots, places, rows, factors, up_run):
    vmem = pl.BlockSpec(memory_space=pltpu.VMEM)
    run, ranks = factors[0].shape[2] - up_run, factors[0].shape[3]
    send = jax.ShapeDtypeStruct((BLK + 2 * planes * up_run, ranks), rows[0].dtype)
    return pl.pallas_call(
        lambda *refs: shrink_kernel(planes, slots, run, *refs),
        out_shape=[jax.ShapeDtypeStruct((BLK, ranks), jnp.float32)]
        + [send] * (PLANE - 1)
        + [jax.ShapeDtypeStruct((planes, 2, up_run, ranks), factors[0].dtype)],
        in_specs=[pl.BlockSpec(memory_space=pltpu.SMEM)] + [vmem] * (PLANE + planes),
        out_specs=[vmem] * (PLANE + 1),
        compiler_params=pltpu.CompilerParams(vmem_limit_bytes=10 * 2**20),
        name="shrink",
    )(places, *rows, *factors)


def expand_kernel(own_ref, up_ref, *refs):
    got = refs[: PLANE - 1]
    key_ref, value_ref, factor = refs[PLANE - 1 :]
    column = lax.rem(lax.axis_index("wide"), PLANE)
    planes, _, up_run, ranks = up_ref.shape
    total = own_ref[...]
    factor[:, :, column] = up_ref[...]
    for k in range(1, PLANE):
        total += got[k - 1][pl.ds(0, BLK)].astype(jnp.float32)
        factor[:, :, column ^ k] = got[k - 1][pl.ds(BLK, 2 * planes * up_run)].reshape(up_ref.shape)
    low_rank = total.astype(jnp.bfloat16)
    is_key = lax.broadcasted_iota(jnp.int32, low_rank.shape, 1) < ranks // 2
    zero = jnp.zeros_like(low_rank)
    both = jnp.concatenate(
        [jnp.where(is_key, low_rank, zero), jnp.where(is_key, zero, low_rank)], axis=0
    )
    for half in range(2):
        for p in range(planes):
            delta = lax.dot_general(
                both,
                factor[p, half].reshape(PLANE * up_run, ranks),
                (((1,), (1,)), ((), ())),
                preferred_element_type=jnp.float32,
            ).astype(jnp.bfloat16)
            columns = pl.ds((half * planes + p) * PLANE * up_run, PLANE * up_run)
            key_ref[:, columns] = delta[:BLK]
            value_ref[:, columns] = delta[BLK:]


def expand(own, up, got):
    planes, _, up_run, ranks = up.shape
    columns = 2 * planes * PLANE * up_run
    vmem = pl.BlockSpec(memory_space=pltpu.VMEM)
    return pl.pallas_call(
        expand_kernel,
        out_shape=[jax.ShapeDtypeStruct((BLK, columns), jnp.bfloat16)] * 2,
        in_specs=[vmem] * (PLANE + 1),
        out_specs=[vmem] * 2,
        scratch_shapes=[pltpu.VMEM((planes, 2, PLANE, up_run, ranks), jnp.bfloat16)],
        compiler_params=pltpu.CompilerParams(vmem_limit_bytes=4 * 2**20),
        name="expand",
    )(own, up, *got)


def plane_body(
    tokens,
    adapter_down_weight,
    adapter_up_weight,
    adapter_entry,
    adapter_of_request,
    token_blocks_per_request,
):
    planes = lax.axis_size("wide") // PLANE
    places, many, *sends = prepare(
        planes,
        tokens,
        adapter_down_weight,
        adapter_up_weight,
        adapter_entry,
        adapter_of_request,
        token_blocks_per_request,
    )
    factors, rows = sends[:planes], sends[planes:]
    beside = swap(rows[1], 1)

    def rest(slots, places, factors, rows, beside):
        factors = [factors[0]] + [swap(factors[d][:slots], d * PLANE) for d in range(1, planes)]
        rows = [rows[0], beside] + [swap(rows[k], k) for k in range(2, PLANE)]
        own, *sends, ups = shrink(planes, slots, places, rows, factors, adapter_up_weight.shape[2])
        got = [swap(sends[k - 1], k) for k in range(1, PLANE)]
        return tuple(expand(own, ups, got))

    return lax.switch(
        many[0],
        [lambda *operands: rest(USUAL, *operands), lambda *operands: rest(SLOTS, *operands)],
        places,
        factors,
        rows,
        beside,
    )


def solution(mesh):
    by_plane = mesh.shape["wide"] == 16 and mesh.shape["narrow"] == 1
    return jax.shard_map(
        plane_body if by_plane else direct_body,
        mesh=mesh,
        in_specs=(
            P(("groups", "wide"), "narrow"),
            P(None, "narrow", "wide", None),
            P(None, "narrow", "wide", None),
            P(),
            P("groups"),
            P("groups"),
        ),
        out_specs=(P(("groups", "wide"), "narrow"), P(("groups", "wide"), "narrow")),
        check_vma=False,
    )
```

time: 55.5 us -> 48.6 us (0.88)
  starting transfers between devices: 21.4 us -> 9.88 us
  waiting for transfers between devices: 21.9 us -> 31.1 us
  local copies, waits for them, and re-layouts: 2.61 us -> 0.06 us
  Pallas kernels: 8.02 us -> 6.08 us
    ppermute x9, starting transfers between devices: 21.4 us -> 9.88 us  [swap(): return lax.ppermute(value, 'wide', [(i, i ^ step) for i in range(count)])]
    ppermute x9, waiting for transfers between devices: 21.9 us -> 31.1 us  [swap(): return lax.ppermute(value, 'wide', [(i, i ^ step) for i in range(count)])]
    unnamed x12 -> x0, local copies, waits for them, and re-layouts: 1.97 us -> none
    pallas_call x1, Pallas kernels: 3.22 us -> 1.26 us  [shrink(): pl.pallas_call(lambda *refs: shrink_kernel(planes, slots, run, *refs), ou...]
    slice x4 -> x3, local copies, waits for them, and re-layouts: 0.64 us -> 0.06 us  [rest(): factors[d][:slots]]
where the time goes in v2:
time: 48.6 us; the launch traced here: 48.4 us
  waiting for transfers between devices  31.1 us (64%)
  starting transfers between devices  9.88 us (20%)
  Pallas kernels  6.08 us (13%)
  between operations  1.29 us (3%)
    ppermute x9, waiting for transfers between devices, swap(): return lax.ppermute(value, 'wide', [(i, i ^ step) for i in range(count)])  31.1 us
    ppermute x9, starting transfers between devices, swap(): return lax.ppermute(value, 'wide', [(i, i ^ step) for i in range(count)])  9.88 us
    pallas_call x1, Pallas kernels, prepare(): pl.pallas_call(lambda *refs: prepare_kernel(planes, *refs), out_shape=[ja...  3.72 us
    pallas_call x1, Pallas kernels, shrink(): pl.pallas_call(lambda *refs: shrink_kernel(planes, slots, run, *refs), ou...  1.26 us
    pallas_call x1, Pallas kernels, expand(): pl.pallas_call(expand_kernel, out_shape=[jax.ShapeDtypeStruct((BLK, colum...  1.1 us
  transfers between devices with their start and end apart: 9, of which 5 were waited for; matrix products, arithmetic and copies ran while one was open for 0% of the time, Pallas kernels for 0%

profile of v2, /device:TPU:0, one launch (start us, length us, event | category | flops | bytes accessed | tf_op | source)
XLA Modules:
  0.0 48.4 jit_solution(512533206517742991)
XLA Ops:
  0.6 3.7 %prepare.1 = (s32[4]{0:T(128)S(1)}, s32[1]{0:T(128)}, bf16[3,2,288,128]{3,2,1,0:T(8,128)(2,1)S(1)}, bf16[3,2,288,128]{3,2,1,0:T(8,128)(2,1)S(1)}, bf16[3,2,288,1...) custom-call(s32[16]{0:T(128)} %refs_0_.1, ...), custom_call_target="tpu_custom_call" | custom-call | tf_op jit(solution)/shard_map/prepare/pallas_call | solution.py:201
  4.4 0.5 %collective-permute-start.16 = (bf16[8,128,256]{2,1,0:T(8,128)(2,1)}, bf16[8,128,256]{2,1,0:T(8,128)(2,1)S(1)}, u32[]{:S(2)}, u32[]{:S(2)}) collective-permute-start(bf16[8,128,256]{2,1,0:T(8,128)(2,1)} %get-tuple-element.84), channel_id=1, source_target_pairs={{0,1},{1,0},{2,3},{3,2},{4,5},{5,4},{6,7},{7,6},{8,9},{9,8},{10,11... | collective-permute-start | bytes 1572872 | tf_op jit(solution)/shard_map/ppermute | solution.py:88
  5.5 1.1 %collective-permute-done.16 = bf16[8,128,256]{2,1,0:T(8,128)(2,1)S(1)} collective-permute-done((bf16[8,128,256]{2,1,0:T(8,128)(2,1)}, bf16[8,128,256]{2,1,0:T(8,128)(2,1)S(1)}, u32[]{:S(2)}, u32[]{:S(2)}) %collective-permute-start.16) | collective-permute-done | bytes 524320 | tf_op jit(solution)/shard_map/ppermute | solution.py:88
  6.6 41.8 %conditional.1 = ((bf16[128,1024]{1,0:T(8,128)(2,1)}, bf16[128,1024]{1,0:T(8,128)(2,1)})) conditional(s32[]{:T(128)} %bitcast, (bf16[8,128,256]{2,1,0:T(8,128)(2,1)S(1)}, bf16[8,128,256]{2,1,0:T(8,128)(2,1)S(1)}, bf16[3,2,288,128]{3,2,1,0:T(8,128)(2,1)S(1)}, bf16[3,2,288,128]{3,2,1,0:T(8,128)(2,1)S(1)}, bf16[3,2,288,128]{3,2,1,0:T(8,128)(2,1)S(1)}, ...), branch_computations={%region_0.0_spmd, %region_1.0_spmd} | conditional | bytes 10682696 | solution.py:343
  6.6 2.9 %collective-permute-start = (bf16[8,128,256]{2,1,0:T(8,128)(2,1)S(1)}, bf16[8,128,256]{2,1,0:T(8,128)(2,1)S(1)}, u32[]{:S(2)}, u32[]{:S(2)}) collective-permute-start(bf16[8,128,256]{2,1,0:T(8,128)(2,1)S(1)} %get-tuple-element.39), channel_id=1, source_target_pairs={{0,2},{1,3},{2,0},{3,1},{4,6},{5,7},{6,4},{7,5},{8,10},{9,11},{10,... | collective-permute-start | bytes 1572872 | tf_op jit(solution)/shard_map/cond/branch_0_fun/ppermute | solution.py:88
  9.5 0.0 collective-permute-start.1
  9.5 3.7 %collective-permute-start.4 = (bf16[2,2,288,128]{3,2,1,0:T(8,128)(2,1)S(1)}, bf16[2,2,288,128]{3,2,1,0:T(8,128)(2,1)S(1)}, u32[]{:S(2)}, u32[]{:S(2)}) collective-permute-start(bf16[2,2,288,128]{3,2,1,0:T(8,128)(2,1)S(1)} %slice.8), channel_id=1, source_target_pairs={{0,12},{1,13},{2,14},{3,15},{4,8},{5,9},{6,10},{7,11},{8,4},{9,5},... | collective-permute-start | bytes 884744 | tf_op jit(solution)/shard_map/cond/branch_0_fun/ppermute | solution.py:88
  13.2 0.1 collective-permute-start.3
  13.3 0.8 %collective-permute-start.2 = (bf16[2,2,288,128]{3,2,1,0:T(8,128)(2,1)S(1)}, bf16[2,2,288,128]{3,2,1,0:T(8,128)(2,1)S(1)}, u32[]{:S(2)}, u32[]{:S(2)}) collective-permute-start(bf16[2,2,288,128]{3,2,1,0:T(8,128)(2,1)S(1)} %slice.6), channel_id=1, source_target_pairs={{0,4},{1,5},{2,6},{3,7},{4,0},{5,1},{6,2},{7,3},{8,12},{9,13},{10,... | collective-permute-start | bytes 884744 | tf_op jit(solution)/shard_map/cond/branch_0_fun/ppermute | solution.py:88
  14.1 7.3 %collective-permute-done.4.refs_8_ = bf16[2,2,288,128]{3,2,1,0:T(8,128)(2,1)S(1)} collective-permute-done((bf16[2,2,288,128]{3,2,1,0:T(8,128)(2,1)S(1)}, bf16[2,2,288,128]{3,2,1,0:T(8,128)(2,1)S(1)}, u32[]{:S(2)}, u32[]{:S(2)}) %collective-permute-start.4) | collective-permute-done | bytes 294944 | tf_op jit(solution)/shard_map/cond/branch_0_fun/ppermute | solution.py:88
  21.4 17.7 %collective-permute-done.3.refs_7_ = bf16[2,2,288,128]{3,2,1,0:T(8,128)(2,1)S(1)} collective-permute-done((bf16[2,2,288,128]{3,2,1,0:T(8,128)(2,1)S(1)}, bf16[2,2,288,128]{3,2,1,0:T(8,128)(2,1)S(1)}, u32[]{:S(2)}, u32[]{:S(2)}) %collective-permute-start.3) | collective-permute-done | bytes 294944 | tf_op jit(solution)/shard_map/cond/branch_0_fun/ppermute | solution.py:88
  39.1 0.0 collective-permute-done.2.refs_6_
  39.1 0.0 collective-permute-done.refs_3_
  39.1 0.0 collective-permute-done.1.refs_4_
  39.1 1.3 %shrink.2 = (f32[128,128]{1,0:T(8,128)S(1)}, bf16[384,128]{1,0:T(8,128)(2,1)S(1)}, bf16[384,128]{1,0:T(8,128)(2,1)S(1)}, bf16[384,128]{1,0:T(8,128)(2,1)S(1)}, bf16[4,2,32,128]{3,2,1,0:T(8,128)(2,1)S(1)}) custom-call(s32[4]{0:T(128)S(1)} %get-tuple-element.36.refs_0_, bf16[8,128,256]{2,1,0:T(8,128)(2,1)S(1)} %get-tuple-element.37.refs_1_, ...), custom_call_target="tpu_custom_call" | custom-call | tf_op jit(solution)/shard_map/cond/branch_0_fun/shrink/pallas_call | solution.py:259
  40.4 0.1 collective-permute-start.5
  40.5 1.6 %collective-permute-start.6 = (bf16[384,128]{1,0:T(8,128)(2,1)S(1)}, bf16[384,128]{1,0:T(8,128)(2,1)S(1)}, u32[]{:S(2)}, u32[]{:S(2)}) collective-permute-start(bf16[384,128]{1,0:T(8,128)(2,1)S(1)} %get-tuple-element.48), channel_id=1, source_target_pairs={{0,2},{1,3},{2,0},{3,1},{4,6},{5,7},{6,4},{7,5},{8,10},{9,11},{10,... | collective-permute-start | bytes 294920 | tf_op jit(solution)/shard_map/cond/branch_0_fun/ppermute | solution.py:88
  42.0 0.3 collective-permute-start.7
  42.3 0.0 collective-permute-done.5.refs_0_
  42.3 3.8 %collective-permute-done.6.refs_1_ = bf16[384,128]{1,0:T(8,128)(2,1)S(1)} collective-permute-done((bf16[384,128]{1,0:T(8,128)(2,1)S(1)}, bf16[384,128]{1,0:T(8,128)(2,1)S(1)}, u32[]{:S(2)}, u32[]{:S(2)}) %collective-permute-start.6) | collective-permute-done | bytes 98336 | tf_op jit(solution)/shard_map/cond/branch_0_fun/ppermute | solution.py:88
  46.1 1.2 %collective-permute-done.7.refs_2_ = bf16[384,128]{1,0:T(8,128)(2,1)S(1)} collective-permute-done((bf16[384,128]{1,0:T(8,128)(2,1)S(1)}, bf16[384,128]{1,0:T(8,128)(2,1)S(1)}, u32[]{:S(2)}, u32[]{:S(2)}) %collective-permute-start.7) | collective-permute-done | bytes 98336 | tf_op jit(solution)/shard_map/cond/branch_0_fun/ppermute | solution.py:88
  47.3 1.1 %expand.2 = (bf16[128,1024]{1,0:T(8,128)(2,1)}, bf16[128,1024]{1,0:T(8,128)(2,1)}) custom-call(f32[128,128]{1,0:T(8,128)S(1)} %get-tuple-element.45.own_ref, bf16[4,2,32,128]{3,2,1,0:T(8,128)(2,1)S(1)} %get-tuple-element.46.up_ref, bf16[384,128]{1,0:T(8,128)(2,1)S(1)} %collective-permute-done.5.refs_0_, bf16[384,128]{1,0:T(8,128)(2,1)S(1)} %collective-permute-done.6.refs_1_, ...), custom_call_target="tpu_custom_call" | custom-call | tf_op jit(solution)/shard_map/cond/branch_0_fun/expand/pallas_call | solution.py:304
  (3 shorter events, 0.1 us)
Async XLA Ops:
  4.4 2.3 %collective-permute-start.16 = (bf16[8,128,256]{2,1,0:T(8,128)(2,1)}, bf16[8,128,256]{2,1,0:T(8,128)(2,1)S(1)}, u32[]{:S(2)}, u32[]{:S(2)}) collective-permute-start(bf16[8,128,256]{2,1,0:T(8,128)(2,1)} %get-tuple-element.84), channel_id=1, source_target_pairs={{0,1},{1,0},{2,3},{3,2},{4,5},{5,4},{6,7},{7,6},{8,9},{9,8},{10,11... | collective-permute-start | bytes 1572872 | tf_op jit(solution)/shard_map/ppermute | solution.py:88
  6.6 32.5 %collective-permute-start = (bf16[8,128,256]{2,1,0:T(8,128)(2,1)S(1)}, bf16[8,128,256]{2,1,0:T(8,128)(2,1)S(1)}, u32[]{:S(2)}, u32[]{:S(2)}) collective-permute-start(bf16[8,128,256]{2,1,0:T(8,128)(2,1)S(1)} %get-tuple-element.39), channel_id=1, source_target_pairs={{0,2},{1,3},{2,0},{3,1},{4,6},{5,7},{6,4},{7,5},{8,10},{9,11},{10,... | collective-permute-start | bytes 1572872 | tf_op jit(solution)/shard_map/cond/branch_0_fun/ppermute | solution.py:88
  9.5 29.6 %collective-permute-start.1 = (bf16[8,128,256]{2,1,0:T(8,128)(2,1)S(1)}, bf16[8,128,256]{2,1,0:T(8,128)(2,1)S(1)}, u32[]{:S(2)}, u32[]{:S(2)}) collective-permute-start(bf16[8,128,256]{2,1,0:T(8,128)(2,1)S(1)} %get-tuple-element.40), channel_id=1, source_target_pairs={{0,3},{1,2},{2,1},{3,0},{4,7},{5,6},{6,5},{7,4},{8,11},{9,10},{10,... | collective-permute-start | bytes 1572872 | tf_op jit(solution)/shard_map/cond/branch_0_fun/ppermute | solution.py:88
  9.5 11.9 %collective-permute-start.4 = (bf16[2,2,288,128]{3,2,1,0:T(8,128)(2,1)S(1)}, bf16[2,2,288,128]{3,2,1,0:T(8,128)(2,1)S(1)}, u32[]{:S(2)}, u32[]{:S(2)}) collective-permute-start(bf16[2,2,288,128]{3,2,1,0:T(8,128)(2,1)S(1)} %slice.8), channel_id=1, source_target_pairs={{0,12},{1,13},{2,14},{3,15},{4,8},{5,9},{6,10},{7,11},{8,4},{9,5},... | collective-permute-start | bytes 884744 | tf_op jit(solution)/shard_map/cond/branch_0_fun/ppermute | solution.py:88
  13.2 25.9 %collective-permute-start.3 = (bf16[2,2,288,128]{3,2,1,0:T(8,128)(2,1)S(1)}, bf16[2,2,288,128]{3,2,1,0:T(8,128)(2,1)S(1)}, u32[]{:S(2)}, u32[]{:S(2)}) collective-permute-start(bf16[2,2,288,128]{3,2,1,0:T(8,128)(2,1)S(1)} %slice.7), channel_id=1, source_target_pairs={{0,8},{1,9},{2,10},{3,11},{4,12},{5,13},{6,14},{7,15},{8,0},{9,1},... | collective-permute-start | bytes 884744 | tf_op jit(solution)/shard_map/cond/branch_0_fun/ppermute | solution.py:88
  13.3 25.8 %collective-permute-start.2 = (bf16[2,2,288,128]{3,2,1,0:T(8,128)(2,1)S(1)}, bf16[2,2,288,128]{3,2,1,0:T(8,128)(2,1)S(1)}, u32[]{:S(2)}, u32[]{:S(2)}) collective-permute-start(bf16[2,2,288,128]{3,2,1,0:T(8,128)(2,1)S(1)} %slice.6), channel_id=1, source_target_pairs={{0,4},{1,5},{2,6},{3,7},{4,0},{5,1},{6,2},{7,3},{8,12},{9,13},{10,... | collective-permute-start | bytes 884744 | tf_op jit(solution)/shard_map/cond/branch_0_fun/ppermute | solution.py:88
  40.4 1.9 %collective-permute-start.5 = (bf16[384,128]{1,0:T(8,128)(2,1)S(1)}, bf16[384,128]{1,0:T(8,128)(2,1)S(1)}, u32[]{:S(2)}, u32[]{:S(2)}) collective-permute-start(bf16[384,128]{1,0:T(8,128)(2,1)S(1)} %get-tuple-element.47), channel_id=1, source_target_pairs={{0,1},{1,0},{2,3},{3,2},{4,5},{5,4},{6,7},{7,6},{8,9},{9,8},{10,11... | collective-permute-start | bytes 294920 | tf_op jit(solution)/shard_map/cond/branch_0_fun/ppermute | solution.py:88
  40.5 5.7 %collective-permute-start.6 = (bf16[384,128]{1,0:T(8,128)(2,1)S(1)}, bf16[384,128]{1,0:T(8,128)(2,1)S(1)}, u32[]{:S(2)}, u32[]{:S(2)}) collective-permute-start(bf16[384,128]{1,0:T(8,128)(2,1)S(1)} %get-tuple-element.48), channel_id=1, source_target_pairs={{0,2},{1,3},{2,0},{3,1},{4,6},{5,7},{6,4},{7,5},{8,10},{9,11},{10,... | collective-permute-start | bytes 294920 | tf_op jit(solution)/shard_map/cond/branch_0_fun/ppermute | solution.py:88
  42.0 5.3 %collective-permute-start.7 = (bf16[384,128]{1,0:T(8,128)(2,1)S(1)}, bf16[384,128]{1,0:T(8,128)(2,1)S(1)}, u32[]{:S(2)}, u32[]{:S(2)}) collective-permute-start(bf16[384,128]{1,0:T(8,128)(2,1)S(1)} %get-tuple-element.49), channel_id=1, source_target_pairs={{0,3},{1,2},{2,1},{3,0},{4,7},{5,6},{6,5},{7,4},{8,11},{9,10},{10,... | collective-permute-start | bytes 294920 | tf_op jit(solution)/shard_map/cond/branch_0_fun/ppermute | solution.py:88

commit v3 on v0

--- a/solution.py
+++ b/solution.py
@@ -1,9 +1,14 @@
 import jax
 import jax.numpy as jnp
 from jax import lax
+from jax.experimental import pallas as pl
+from jax.experimental.pallas import tpu as pltpu
 from jax.sharding import PartitionSpec as P
 
 BLK = 128
+PLANE = 4
+SLOTS = 3
+USUAL = 2
 
 
 def block_tables(
@@ -27,7 +32,7 @@
     return jnp.sum(slot_table * adapter_entry[None, :], axis=1)
 
 
-def body(
+def direct_body(
     tokens,
     adapter_down_weight,
     adapter_up_weight,
@@ -78,9 +83,365 @@
     return (key_delta, value_delta)
 
 
+def swap(value, step):
+    count = lax.axis_size("wide")
+    return lax.ppermute(value, "wide", [(i, i ^ step) for i in range(count)])
+
+
+def swap_cores(value):
+    count = lax.axis_size("wide")
+    pairs = [[i, i + 1] for i in range(0, count, 2)]
+    return lax.all_to_all(value, "wide", 0, 0, axis_index_groups=pairs, tiled=True)
+
+
+def pick(index, values):
+    got = values[0]
+    for i in range(1, len(values)):
+        got = jnp.where(index == i, values[i], got)
+    return got
+
+
+def slices(tokens_ref, column, run, out, sem):
+    return [
+        pltpu.make_async_copy(
+            tokens_ref.at[:, pl.ds(pl.multiple_of((piece * PLANE + column) * run, run), run)],
+            out.at[piece],
+            sem.at[piece],
+        )
+        for piece in range(out.shape[0])
+    ]
+
+
+def choose_kernel(
+    planes, entry_hbm, adapter_hbm, counts_hbm, tokens_ref, down_ref, up_ref, table_ref, *refs
+):
+    others = planes - 2
+    sends, tokens_out = refs[:others], refs[others : others + PLANE - 2]
+    entry_ref, adapter_ref, counts_ref, small_sem, tokens_sem, sem = refs[others + PLANE - 2 :]
+    me = lax.axis_index("wide")
+    column, plane = lax.rem(me, PLANE), lax.div(me, PLANE)
+    run, up_run = down_ref.shape[2], up_ref.shape[2]
+    small = [
+        pltpu.make_async_copy(entry_hbm, entry_ref, small_sem.at[0]),
+        pltpu.make_async_copy(adapter_hbm, adapter_ref, small_sem.at[1]),
+        pltpu.make_async_copy(counts_hbm, counts_ref, small_sem.at[2]),
+    ]
+    for copy in small:
+        copy.start()
+    copies = []
+    for k, out in enumerate(tokens_out):
+        copies += slices(tokens_ref, column ^ (k + 2), run, out, tokens_sem.at[k])
+    for copy in copies:
+        copy.start()
+    for copy in small:
+        copy.wait()
+
+    requests = counts_ref.shape[0]
+    ends, total = [], 0
+    for q in range(requests):
+        total = total + counts_ref[q]
+        ends.append(total)
+    entries = [entry_ref[adapter_ref[q]] for q in range(requests)]
+
+    def listed(p):
+        ids = []
+        for i in range(PLANE):
+            block = p * PLANE + jnp.where(p % 2 == 0, i, PLANE - 1 - i)
+            got = entries[0]
+            for q in range(1, requests):
+                got = jnp.where(ends[q - 1] <= block, entries[q], got)
+            ids.append(got)
+        place, held, count = [jnp.int32(0)], [ids[0]] * SLOTS, jnp.int32(1)
+        for i in range(1, PLANE):
+            found = count
+            for j in range(i):
+                found = jnp.where(ids[i] == ids[j], place[j], found)
+            place.append(found)
+            held = [jnp.where(found == s, ids[i], held[s]) for s in range(SLOTS)]
+            count = jnp.maximum(count, found + 1)
+        return held, place, count
+
+    most = jnp.int32(1)
+    for d in reversed(range(planes)):
+        held, place, count = listed(plane ^ d)
+        most = jnp.maximum(most, count)
+        if d > 1:
+            for s in range(USUAL):
+                out = sends[d - 2].at[s]
+                for part, (ref, at) in enumerate(
+                    ((down_ref, pl.ds(0, run)), (up_ref, pl.ds(run, up_run)))
+                ):
+                    copies.append(
+                        pltpu.make_async_copy(ref.at[held[s]], out.at[:, at], sem.at[d - 2, s, part])
+                    )
+                    copies[-1].start()
+        else:
+            for s in range(SLOTS):
+                table_ref[PLANE + d * SLOTS + s] = held[s]
+    for k in range(PLANE):
+        i = column ^ k
+        table_ref[k] = pick(jnp.where(plane % 2 == 0, i, PLANE - 1 - i), place)
+    table_ref[PLANE + 2 * SLOTS] = jnp.where(most > USUAL, 1, 0)
+    for copy in copies:
+        copy.wait()
+
+
+def choose(planes, tokens, down, up, entry, adapter, counts):
+    hbm = pl.BlockSpec(memory_space=pltpu.HBM)
+    others = planes - 2
+    send = jax.ShapeDtypeStruct((USUAL, 2, down.shape[2] + up.shape[2], down.shape[3]), down.dtype)
+    return pl.pallas_call(
+        lambda *refs: choose_kernel(planes, *refs),
+        out_shape=[jax.ShapeDtypeStruct((PLANE + 2 * SLOTS + 1,), jnp.int32)]
+        + [send] * others
+        + [jax.ShapeDtypeStruct((2 * planes, BLK, down.shape[2]), tokens.dtype)] * (PLANE - 2),
+        in_specs=[hbm] * 6,
+        out_specs=[pl.BlockSpec(memory_space=pltpu.SMEM)]
+        + [pl.BlockSpec(memory_space=pltpu.VMEM)] * (others + PLANE - 2),
+        scratch_shapes=[
+            pltpu.SMEM(entry.shape, jnp.int32),
+            pltpu.SMEM(adapter.shape, jnp.int32),
+            pltpu.SMEM(counts.shape, jnp.int32),
+            pltpu.SemaphoreType.DMA((3,)),
+            pltpu.SemaphoreType.DMA((PLANE - 2, 2 * planes)),
+            pltpu.SemaphoreType.DMA((others, USUAL, 2)),
+        ],
+        compiler_params=pltpu.CompilerParams(vmem_limit_bytes=57 * 2**20),
+        name="choose",
+    )(entry, adapter, counts, tokens, down, up)
+
+
+def gather_kernel(planes, table_ref, tokens_ref, down_ref, up_ref, own_ref, near_ref, pair_ref, tokens_sem, sem):
+    column = lax.rem(lax.axis_index("wide"), PLANE)
+    run, up_run = down_ref.shape[2], up_ref.shape[2]
+    copies = []
+    for core in range(2):
+        at = lax.div(column, 2) * 2 + core
+        copies += slices(tokens_ref, at, run, pair_ref.at[core], tokens_sem.at[core])
+    for d, out in enumerate((own_ref, near_ref)):
+        for s in range(out.shape[0]):
+            slot = table_ref[PLANE + d * SLOTS + s]
+            copies.append(
+                pltpu.make_async_copy(
+                    down_ref.at[slot], out.at[s, :, pl.ds(0, run)], sem.at[d, s, 0]
+                )
+            )
+            copies.append(
+                pltpu.make_async_copy(
+                    up_ref.at[slot], out.at[s, :, pl.ds(run, up_run)], sem.at[d, s, 1]
+                )
+            )
+    for copy in copies:
+        copy.start()
+    for copy in copies:
+        copy.wait()
+
+
+def gather(planes, table, tokens, down, up):
+    run = down.shape[2]
+    hbm = pl.BlockSpec(memory_space=pltpu.HBM)
+    rows = (2, run + up.shape[2], down.shape[3])
+    return pl.pallas_call(
+        lambda *refs: gather_kernel(planes, *refs),
+        out_shape=[
+            jax.ShapeDtypeStruct((SLOTS,) + rows, down.dtype),
+            jax.ShapeDtypeStruct((USUAL,) + rows, down.dtype),
+        ]
+        + [jax.ShapeDtypeStruct((2, 2 * planes, BLK, run), tokens.dtype)],
+        in_specs=[pl.BlockSpec(memory_space=pltpu.SMEM)] + [hbm] * 3,
+        out_specs=[pl.BlockSpec(memory_space=pltpu.VMEM)] * 3,
+        scratch_shapes=[
+            pltpu.SemaphoreType.DMA((2, 2 * planes)),
+            pltpu.SemaphoreType.DMA((2, SLOTS, 2)),
+        ],
+        compiler_params=pltpu.CompilerParams(vmem_limit_bytes=57 * 2**20),
+        cost_estimate=pl.CostEstimate(flops=10**10, bytes_accessed=0, transcendentals=0),
+        name="gather",
+    )(table, tokens, down, up)
+
+
+def up_rows(factors, distances, place):
+    rows = []
+    for d in distances:
+        slot = jnp.minimum(place, factors[d].shape[0] - 1)
+        rows += [factors[d][slot, half] for half in range(2)]
+    return rows
+
+
+def shrink(planes, slots, run, blocks, near, far, places, rows, factors, held=(), ups=None, flops=None, kept=(), flag=False):
+    vmem = pl.BlockSpec(memory_space=pltpu.VMEM)
+    up_run, ranks = factors[0].shape[2] - run, factors[0].shape[3]
+
+    def kernel(places_ref, *refs):
+        row_refs, refs = refs[: len(rows)], refs[len(rows) :]
+        factor_refs, refs = refs[: len(factors)], refs[len(factors) :]
+        held_refs, outs = list(refs[: len(held)]), refs[len(held) + len(kept) :]
+        me = lax.axis_index("wide")
+        core, plane = lax.rem(me, 2), lax.div(me, PLANE)
+        at = [places_ref[k] for k in blocks]
+        views = [ref.at[:, :, pl.ds(run, up_run)] for ref in factor_refs]
+
+        def rows_at(k, piece):
+            return row_refs[0][core ^ k, piece] if k < 2 else row_refs[k - 1][piece]
+
+        def sums_of(chosen, distances):
+            total = jnp.zeros((len(chosen) * BLK, slots * ranks), jnp.float32)
+            for d in distances:
+                for half in range(2):
+                    piece = half * planes + (plane ^ d)
+                    total += jnp.dot(
+                        jnp.concatenate([rows_at(blocks[i], piece) for i in chosen], axis=0),
+                        jnp.concatenate(
+                            [factor_refs[d][s, half, pl.ds(0, run)] for s in range(slots)], axis=1
+                        ),
+                        preferred_element_type=jnp.float32,
+                    )
+            parts = [total[j * BLK : (j + 1) * BLK] for j in range(len(chosen))]
+            return {
+                i: pick(at[i], [part[:, s * ranks : (s + 1) * ranks] for s in range(slots)])
+                for i, part in zip(chosen, parts)
+            }
+
+        if flag:
+            *outs, flag_ref = outs
+            flag_ref[0] = places_ref[PLANE + 2 * SLOTS]
+        every = range(len(blocks))
+        mine = sums_of(every, far) if far else {}
+        here = [i for i in every if blocks[i] in near]
+        for i, part in (sums_of(here, (0,)) if here else {}).items():
+            mine[i] = mine[i] + part if far else part
+        for i in every:
+            if i not in here:
+                mine[i] = mine[i] + held_refs.pop(0)[...]
+            outs[i][pl.ds(0, BLK)] = mine[i].astype(outs[i].dtype)
+            for j, part in enumerate(up_rows(views, ups or (), at[i])):
+                outs[i][pl.ds(BLK + j * up_run, up_run)] = part.astype(outs[i].dtype)
+
+    height = BLK + len(ups or ()) * 2 * up_run
+    exact = [ups is None or k == 0 for k in blocks]
+    cost = None
+    if flops is not None:
+        cost = pl.CostEstimate(flops=flops, bytes_accessed=0, transcendentals=0)
+    return pl.pallas_call(
+        kernel,
+        out_shape=[
+            jax.ShapeDtypeStruct((height, ranks), jnp.float32 if full else rows[0].dtype)
+            for full in exact
+        ]
+        + [jax.ShapeDtypeStruct((1,), jnp.int32)] * flag,
+        in_specs=[pl.BlockSpec(memory_space=pltpu.SMEM)]
+        + [vmem] * (len(rows) + len(factors) + len(held))
+        + [pl.BlockSpec(memory_space=pl.ANY)] * len(kept),
+        out_specs=[vmem] * len(blocks) + [pl.BlockSpec(memory_space=pltpu.SMEM)] * flag,
+        compiler_params=pltpu.CompilerParams(vmem_limit_bytes=10 * 2**20),
+        cost_estimate=cost,
+        name="shrink",
+    )(places, *rows, *factors, *held, *kept)
+
+
+def expand(planes, up_run, sums):
+    ranks = sums[0].shape[1]
+    columns = 2 * planes * PLANE * up_run
+    vmem = pl.BlockSpec(memory_space=pltpu.VMEM)
+    span = 2 * up_run
+
+    def kernel(*refs):
+        sum_refs = refs[:PLANE]
+        key_ref, value_ref, factor = refs[PLANE:]
+        me = lax.axis_index("wide")
+        column, plane = lax.rem(me, PLANE), lax.div(me, PLANE)
+        total = jnp.zeros((BLK, ranks), jnp.float32)
+        for k in range(PLANE):
+            total += sum_refs[k][pl.ds(0, BLK)].astype(jnp.float32)
+            for d in range(planes):
+                rows = sum_refs[k][pl.ds(BLK + d * span, span)]
+                factor[plane ^ d, :, column ^ k] = rows.astype(factor.dtype).reshape(2, up_run, ranks)
+        low_rank = total.astype(jnp.bfloat16)
+        is_key = lax.broadcasted_iota(jnp.int32, low_rank.shape, 1) < ranks // 2
+        zero = jnp.zeros_like(low_rank)
+        both = jnp.concatenate(
+            [jnp.where(is_key, low_rank, zero), jnp.where(is_key, zero, low_rank)], axis=0
+        )
+        for half in range(2):
+            for p in range(planes):
+                delta = lax.dot_general(
+                    both,
+                    factor[p, half].reshape(PLANE * up_run, ranks),
+                    (((1,), (1,)), ((), ())),
+                    preferred_element_type=jnp.float32,
+                ).astype(jnp.bfloat16)
+                at = pl.ds((half * planes + p) * PLANE * up_run, PLANE * up_run)
+                key_ref[:, at] = delta[:BLK]
+                value_ref[:, at] = delta[BLK:]
+
+    return pl.pallas_call(
+        kernel,
+        out_shape=[jax.ShapeDtypeStruct((BLK, columns), jnp.bfloat16)] * 2,
+        in_specs=[vmem] * PLANE,
+        out_specs=[vmem] * 2,
+        scratch_shapes=[pltpu.VMEM((planes, 2, PLANE, up_run, ranks), jnp.bfloat16)],
+        compiler_params=pltpu.CompilerParams(vmem_limit_bytes=4 * 2**20),
+        name="expand",
+    )(*sums)
+
+
+def plane_body(
+    tokens,
+    adapter_down_weight,
+    adapter_up_weight,
+    adapter_entry,
+    adapter_of_request,
+    token_blocks_per_request,
+):
+    planes = lax.axis_size("wide") // PLANE
+    places, *sends = choose(
+        planes,
+        tokens,
+        adapter_down_weight,
+        adapter_up_weight,
+        adapter_entry,
+        adapter_of_request,
+        token_blocks_per_request,
+    )
+    far, across = sends[: planes - 2], sends[planes - 2 :]
+    own_factors, near, pair = gather(planes, places, tokens, adapter_down_weight, adapter_up_weight)
+    sends = sends + [near, pair]
+    run, up_run = adapter_down_weight.shape[2], adapter_up_weight.shape[2]
+    whole, blocks = tuple(range(planes)), tuple(range(PLANE))
+    far = [swap(far[d - 2], d * PLANE) for d in range(2, planes)]
+    factors = [own_factors, swap(near, PLANE)] + far
+    rows = [swap_cores(pair)] + [swap(across[k - 2], k) for k in range(2, PLANE)]
+    *held, many = shrink(
+        planes, SLOTS, run, (0, 1), (0, 1), (), places, rows[:1], factors[:1], flops=None, flag=True
+    )
+
+    def finish(sums):
+        sums = [sums[0]] + [swap(sums[k], k) for k in range(1, PLANE)]
+        return tuple(expand(planes, up_run, sums))
+
+    def usual(places, factors, rows, held, kept):
+        sums = shrink(
+            planes, USUAL, run, blocks, (2, 3), whole[1:], places, rows, factors, held, whole
+        )
+        return finish(sums)
+
+    def more(places, factors, rows, held, kept):
+        third = swap(jnp.concatenate([factors[d ^ 1][:1] for d in whole[1:]]), PLANE)
+        factors = [factors[0]] + [
+            jnp.concatenate([factors[d], third[d - 1 : d]]) for d in whole[1:]
+        ]
+        sums = shrink(
+            planes, SLOTS, run, blocks, (2, 3), whole[1:], places, rows, factors, held, whole, kept=kept
+        )
+        return finish(sums)
+
+    return lax.switch(many[0], [usual, more], places, factors, rows, held, sends)
+
+
 def solution(mesh):
+    by_plane = mesh.shape["wide"] == 16 and mesh.shape["narrow"] == 1
     return jax.shard_map(
-        body,
+        plane_body if by_plane else direct_body,
         mesh=mesh,
         in_specs=(
             P(("groups", "wide"), "narrow"),

time: 79.3 us -> 42.8 us (0.54)
  the two profiles are of different devices: /device:TPU:15 before, /device:TPU:0 now
where the time goes in v3:
time: 42.8 us; the launch traced here: 42.5 us
  waiting for transfers between devices  18.7 us (44%)
  starting transfers between devices  9.25 us (22%)
  Pallas kernels  8.65 us (20%)
  blocking collectives  4.56 us (11%)
  between operations  1.31 us (3%)
    ppermute x8, waiting for transfers between devices, swap(): return lax.ppermute(value, 'wide', [(i, i ^ step) for i in range(count)])  18.7 us
    ppermute x8, starting transfers between devices, swap(): return lax.ppermute(value, 'wide', [(i, i ^ step) for i in range(count)])  9.25 us
    all_to_all x1, blocking collectives, swap_cores(): lax.all_to_all(value, 'wide', 0, 0, axis_index_groups=pairs, tiled=True)  4.56 us
    pallas_call x1, Pallas kernels, choose(): pl.pallas_call(lambda *refs: choose_kernel(planes, *refs), out_shape=[jax...  2.86 us
    pallas_call x1, Pallas kernels, gather(): pl.pallas_call(lambda *refs: gather_kernel(planes, *refs), out_shape=[jax...  2.43 us
    pallas_call x2, Pallas kernels, shrink(): pl.pallas_call(kernel, out_shape=[jax.ShapeDtypeStruct((height, ranks), j...  2.26 us
    pallas_call x1, Pallas kernels, expand(): pl.pallas_call(kernel, out_shape=[jax.ShapeDtypeStruct((BLK, columns), jn...  1.1 us
  transfers between devices with their start and end apart: 8, of which 4 were waited for; matrix products, arithmetic and copies ran while one was open for 0% of the time, Pallas kernels for 8%

profile of v3, /device:TPU:0, one launch (start us, length us, event | category | flops | bytes accessed | tf_op | source)
XLA Modules:
  0.0 42.5 jit_solution(251281526885638844)
XLA Ops:
  0.6 2.9 %choose.1 = (s32[11]{0:T(128)S(1)}, bf16[2,2,288,128]{3,2,1,0:T(8,128)(2,1)S(1)}, bf16[2,2,288,128]{3,2,1,0:T(8,128)(2,1)S(1)}, bf16[8,128,256]{2,1,0:T(8,128)(2,1)S(1)}, bf16[8,128,256]{2,1,0:T(8,128)(2,1)S(1)}) custom-call(s32[16]{0:T(128)} %refs_0_.1, s32[4]{0:T(128)} %refs_1_.2, s32[4]{0:T(128)} %refs_2_.2, bf16[128,8192]{1,0:T(8,128)(2,1)} %refs_1_.3, ...), custom_call_target="tpu_custom_call" | custom-call | tf_op jit(solution)/shard_map/choose/pallas_call | solution.py:193
  3.5 4.2 %collective-permute-start.10 = (bf16[2,2,288,128]{3,2,1,0:T(8,128)(2,1)S(1)}, bf16[2,2,288,128]{3,2,1,0:T(8,128)(2,1)S(1)}, u32[]{:S(2)}, u32[]{:S(2)}) collective-permute-start(bf16[2,2,288,128]{3,2,1,0:T(8,128)(2,1)S(1)} %get-tuple-element.106), channel_id=1, source_target_pairs={{0,8},{1,9},{2,10},{3,11},{4,12},{5,13},{6,14},{7,15},{8,0},{9,1},... | collective-permute-start | bytes 884744 | tf_op jit(solution)/shard_map/ppermute | solution.py:88
  7.7 1.3 %collective-permute-start.11 = (bf16[2,2,288,128]{3,2,1,0:T(8,128)(2,1)S(1)}, bf16[2,2,288,128]{3,2,1,0:T(8,128)(2,1)S(1)}, u32[]{:S(2)}, u32[]{:S(2)}) collective-permute-start(bf16[2,2,288,128]{3,2,1,0:T(8,128)(2,1)S(1)} %get-tuple-element.107), channel_id=1, source_target_pairs={{0,12},{1,13},{2,14},{3,15},{4,8},{5,9},{6,10},{7,11},{8,4},{9,5},... | collective-permute-start | bytes 884744 | tf_op jit(solution)/shard_map/ppermute | solution.py:88
  8.9 1.5 %collective-permute-start.7 = (bf16[8,128,256]{2,1,0:T(8,128)(2,1)S(1)}, bf16[8,128,256]{2,1,0:T(8,128)(2,1)S(1)}, u32[]{:S(2)}, u32[]{:S(2)}) collective-permute-start(bf16[8,128,256]{2,1,0:T(8,128)(2,1)S(1)} %get-tuple-element.103), channel_id=1, source_target_pairs={{0,2},{1,3},{2,0},{3,1},{4,6},{5,7},{6,4},{7,5},{8,10},{9,11},{10,... | collective-permute-start | bytes 1572872 | tf_op jit(solution)/shard_map/ppermute | solution.py:88
  10.4 0.0 collective-permute-start.8
  10.4 2.4 %gather.1 = (bf16[3,2,288,128]{3,2,1,0:T(8,128)(2,1)S(1)}, bf16[2,2,288,128]{3,2,1,0:T(8,128)(2,1)S(1)}, bf16[2,8,128,256]{3,2,1,0:T(8,128)(2,1)S(1)}) custom-call(s32[11]{0:T(128)S(1)} %get-tuple-element.99.refs_0_.places_ref, bf16[128,8192]{1,0:T(8,128)(2,1)} %refs_1_.3, bf16[16,2,256,128]{3,2,1,0:T(8,128)(2,1)} %refs_2_.3, bf16[16,2,32,128]{3,2,1,0:T(8,128)(2,1)} %refs_3_.3), custom_call_target="tpu_custom_call" | custom-call | flops 10000000000 | tf_op jit(solution)/shard_map/gather/pallas_call | solution.py:244
  12.9 0.4 collective-permute-start.9
  13.2 4.6 %all_to_all.5.refs_0_ = bf16[2,8,128,256]{3,2,1,0:T(8,128)(2,1)S(1)} all-to-all(bf16[2,8,128,256]{3,2,1,0:T(8,128)(2,1)S(1)} %get-tuple-element.100), channel_id=1, replica_groups={{0,1},{2,3},{4,5},{6,7},{8,9},{10,11},{12,13},{14,15},{16,17},{18,19},{..., dimensions={0} | all-to-all | bytes 2097152 | tf_op jit(solution)/shard_map/all_to_all | solution.py:94
  17.8 1.1 %shrink.5 = (f32[128,128]{1,0:T(8,128)S(1)}, f32[128,128]{1,0:T(8,128)S(1)}, s32[1]{0:T(128)}) custom-call(s32[11]{0:T(128)S(1)} %get-tuple-element.99.refs_0_.places_ref, bf16[2,8,128,256]{3,2,1,0:T(8,128)(2,1)S(1)} %all_to_all.5.refs_0_, bf16[3,2,288,128]{3,2,1,0:T(8,128)(2,1)S(1)} %get-tuple-element.101.refs_1_), custom_call_target="tpu_custom_call" | custom-call | tf_op jit(solution)/shard_map/shrink/pallas_call | solution.py:325
  19.5 8.6 %collective-permute-done.10 = bf16[2,2,288,128]{3,2,1,0:T(8,128)(2,1)S(1)} collective-permute-done((bf16[2,2,288,128]{3,2,1,0:T(8,128)(2,1)S(1)}, bf16[2,2,288,128]{3,2,1,0:T(8,128)(2,1)S(1)}, u32[]{:S(2)}, u32[]{:S(2)}) %collective-permute-start.10) | collective-permute-done | bytes 294944 | tf_op jit(solution)/shard_map/ppermute | solution.py:88
  28.2 0.0 collective-permute-done.11
  28.2 5.1 %collective-permute-done.9 = bf16[2,2,288,128]{3,2,1,0:T(8,128)(2,1)S(1)} collective-permute-done((bf16[2,2,288,128]{3,2,1,0:T(8,128)(2,1)S(1)}, bf16[2,2,288,128]{3,2,1,0:T(8,128)(2,1)S(1)}, u32[]{:S(2)}, u32[]{:S(2)}) %collective-permute-start.9) | collective-permute-done | bytes 294944 | tf_op jit(solution)/shard_map/ppermute | solution.py:88
  33.3 0.0 collective-permute-done.7
  33.3 0.0 collective-permute-done.8
  33.3 9.2 %conditional.1 = ((bf16[128,1024]{1,0:T(8,128)(2,1)}, bf16[128,1024]{1,0:T(8,128)(2,1)})) conditional(s32[]{:T(128)} %bitcast, (s32[11]{0:T(128)S(1)}, bf16[2,8,128,256]{3,2,1,0:T(8,128)(2,1)S(1)}, bf16[8,128,256]{2,1,0:T(8,128)(2,1)S(1)}, bf16[8,128,256]{2,1,0:T(8,128)(2,1)S(1)}, bf16[3,2,288,128]{3,2,1,0:T(8,128)(2,1)S(1)}, ...), branch_computations={%region_0.0_spmd, %region_1.0_spmd} | conditional | flops 1105920 | bytes 23724480 | solution.py:438
  33.3 1.2 %shrink.3 = (f32[384,128]{1,0:T(8,128)S(1)}, bf16[384,128]{1,0:T(8,128)(2,1)S(1)}, bf16[384,128]{1,0:T(8,128)(2,1)S(1)}, bf16[384,128]{1,0:T(8,128)(2,1)S(1)}) custom-call(s32[11]{0:T(128)S(1)} %get-tuple-element.52.places_ref, bf16[2,8,128,256]{3,2,1,0:T(8,128)(2,1)S(1)} %get-tuple-element.53.refs_0_, bf16[8,128,256]{2,1,0:T(8,128)(2,1)S(1)} %get-tuple-element.54.refs_1_, ...), custom_call_target="tpu_custom_call" | custom-call | tf_op jit(solution)/shard_map/cond/branch_0_fun/shrink/pallas_call | solution.py:325
  34.5 0.2 collective-permute-start
  34.7 1.3 %collective-permute-start.1 = (bf16[384,128]{1,0:T(8,128)(2,1)S(1)}, bf16[384,128]{1,0:T(8,128)(2,1)S(1)}, u32[]{:S(2)}, u32[]{:S(2)}) collective-permute-start(bf16[384,128]{1,0:T(8,128)(2,1)S(1)} %get-tuple-element.64), channel_id=1, source_target_pairs={{0,2},{1,3},{2,0},{3,1},{4,6},{5,7},{6,4},{7,5},{8,10},{9,11},{10,... | collective-permute-start | bytes 294920 | tf_op jit(solution)/shard_map/cond/branch_0_fun/ppermute | solution.py:88
  35.9 0.5 %collective-permute-start.2 = (bf16[384,128]{1,0:T(8,128)(2,1)S(1)}, bf16[384,128]{1,0:T(8,128)(2,1)S(1)}, u32[]{:S(2)}, u32[]{:S(2)}) collective-permute-start(bf16[384,128]{1,0:T(8,128)(2,1)S(1)} %get-tuple-element.65), channel_id=1, source_target_pairs={{0,3},{1,2},{2,1},{3,0},{4,7},{5,6},{6,5},{7,4},{8,11},{9,10},{10,... | collective-permute-start | bytes 294920 | tf_op jit(solution)/shard_map/cond/branch_0_fun/ppermute | solution.py:88
  36.4 0.0 collective-permute-done.refs_1_
  36.4 3.8 %collective-permute-done.1.refs_2_ = bf16[384,128]{1,0:T(8,128)(2,1)S(1)} collective-permute-done((bf16[384,128]{1,0:T(8,128)(2,1)S(1)}, bf16[384,128]{1,0:T(8,128)(2,1)S(1)}, u32[]{:S(2)}, u32[]{:S(2)}) %collective-permute-start.1) | collective-permute-done | bytes 98336 | tf_op jit(solution)/shard_map/cond/branch_0_fun/ppermute | solution.py:88
  40.3 1.2 %collective-permute-done.2.refs_3_ = bf16[384,128]{1,0:T(8,128)(2,1)S(1)} collective-permute-done((bf16[384,128]{1,0:T(8,128)(2,1)S(1)}, bf16[384,128]{1,0:T(8,128)(2,1)S(1)}, u32[]{:S(2)}, u32[]{:S(2)}) %collective-permute-start.2) | collective-permute-done | bytes 98336 | tf_op jit(solution)/shard_map/cond/branch_0_fun/ppermute | solution.py:88
  41.4 1.1 %expand.2 = (bf16[128,1024]{1,0:T(8,128)(2,1)}, bf16[128,1024]{1,0:T(8,128)(2,1)}) custom-call(f32[384,128]{1,0:T(8,128)S(1)} %get-tuple-element.62.refs_0_, bf16[384,128]{1,0:T(8,128)(2,1)S(1)} %collective-permute-done.refs_1_, bf16[384,128]{1,0:T(8,128)(2,1)S(1)} %collective-permute-done.1.refs_2_, bf16[384,128]{1,0:T(8,128)(2,1)S(1)} %collective-permute-done.2.refs_3_), custom_call_target="tpu_custom_call" | custom-call | tf_op jit(solution)/shard_map/cond/branch_0_fun/expand/pallas_call | solution.py:377
Async XLA Ops:
  3.5 24.7 %collective-permute-start.10 = (bf16[2,2,288,128]{3,2,1,0:T(8,128)(2,1)S(1)}, bf16[2,2,288,128]{3,2,1,0:T(8,128)(2,1)S(1)}, u32[]{:S(2)}, u32[]{:S(2)}) collective-permute-start(bf16[2,2,288,128]{3,2,1,0:T(8,128)(2,1)S(1)} %get-tuple-element.106), channel_id=1, source_target_pairs={{0,8},{1,9},{2,10},{3,11},{4,12},{5,13},{6,14},{7,15},{8,0},{9,1},... | collective-permute-start | bytes 884744 | tf_op jit(solution)/shard_map/ppermute | solution.py:88
  7.7 20.5 %collective-permute-start.11 = (bf16[2,2,288,128]{3,2,1,0:T(8,128)(2,1)S(1)}, bf16[2,2,288,128]{3,2,1,0:T(8,128)(2,1)S(1)}, u32[]{:S(2)}, u32[]{:S(2)}) collective-permute-start(bf16[2,2,288,128]{3,2,1,0:T(8,128)(2,1)S(1)} %get-tuple-element.107), channel_id=1, source_target_pairs={{0,12},{1,13},{2,14},{3,15},{4,8},{5,9},{6,10},{7,11},{8,4},{9,5},... | collective-permute-start | bytes 884744 | tf_op jit(solution)/shard_map/ppermute | solution.py:88
  8.9 24.3 %collective-permute-start.7 = (bf16[8,128,256]{2,1,0:T(8,128)(2,1)S(1)}, bf16[8,128,256]{2,1,0:T(8,128)(2,1)S(1)}, u32[]{:S(2)}, u32[]{:S(2)}) collective-permute-start(bf16[8,128,256]{2,1,0:T(8,128)(2,1)S(1)} %get-tuple-element.103), channel_id=1, source_target_pairs={{0,2},{1,3},{2,0},{3,1},{4,6},{5,7},{6,4},{7,5},{8,10},{9,11},{10,... | collective-permute-start | bytes 1572872 | tf_op jit(solution)/shard_map/ppermute | solution.py:88
  10.4 22.8 %collective-permute-start.8 = (bf16[8,128,256]{2,1,0:T(8,128)(2,1)S(1)}, bf16[8,128,256]{2,1,0:T(8,128)(2,1)S(1)}, u32[]{:S(2)}, u32[]{:S(2)}) collective-permute-start(bf16[8,128,256]{2,1,0:T(8,128)(2,1)S(1)} %get-tuple-element.104), channel_id=1, source_target_pairs={{0,3},{1,2},{2,1},{3,0},{4,7},{5,6},{6,5},{7,4},{8,11},{9,10},{10,... | collective-permute-start | bytes 1572872 | tf_op jit(solution)/shard_map/ppermute | solution.py:88
  12.9 20.4 %collective-permute-start.9 = (bf16[2,2,288,128]{3,2,1,0:T(8,128)(2,1)S(1)}, bf16[2,2,288,128]{3,2,1,0:T(8,128)(2,1)S(1)}, u32[]{:S(2)}, u32[]{:S(2)}) collective-permute-start(bf16[2,2,288,128]{3,2,1,0:T(8,128)(2,1)S(1)} %get-tuple-element.105), channel_id=1, source_target_pairs={{0,4},{1,5},{2,6},{3,7},{4,0},{5,1},{6,2},{7,3},{8,12},{9,13},{10,... | collective-permute-start | bytes 884744 | tf_op jit(solution)/shard_map/ppermute | solution.py:88
  34.5 2.0 %collective-permute-start = (bf16[384,128]{1,0:T(8,128)(2,1)S(1)}, bf16[384,128]{1,0:T(8,128)(2,1)S(1)}, u32[]{:S(2)}, u32[]{:S(2)}) collective-permute-start(bf16[384,128]{1,0:T(8,128)(2,1)S(1)} %get-tuple-element.63), channel_id=1, source_target_pairs={{0,1},{1,0},{2,3},{3,2},{4,5},{5,4},{6,7},{7,6},{8,9},{9,8},{10,11... | collective-permute-start | bytes 294920 | tf_op jit(solution)/shard_map/cond/branch_0_fun/ppermute | solution.py:88
  34.7 5.6 %collective-permute-start.1 = (bf16[384,128]{1,0:T(8,128)(2,1)S(1)}, bf16[384,128]{1,0:T(8,128)(2,1)S(1)}, u32[]{:S(2)}, u32[]{:S(2)}) collective-permute-start(bf16[384,128]{1,0:T(8,128)(2,1)S(1)} %get-tuple-element.64), channel_id=1, source_target_pairs={{0,2},{1,3},{2,0},{3,1},{4,6},{5,7},{6,4},{7,5},{8,10},{9,11},{10,... | collective-permute-start | bytes 294920 | tf_op jit(solution)/shard_map/cond/branch_0_fun/ppermute | solution.py:88
  35.9 5.5 %collective-permute-start.2 = (bf16[384,128]{1,0:T(8,128)(2,1)S(1)}, bf16[384,128]{1,0:T(8,128)(2,1)S(1)}, u32[]{:S(2)}, u32[]{:S(2)}) collective-permute-start(bf16[384,128]{1,0:T(8,128)(2,1)S(1)} %get-tuple-element.65), channel_id=1, source_target_pairs={{0,3},{1,2},{2,1},{3,0},{4,7},{5,6},{6,5},{7,4},{8,11},{9,10},{10,... | collective-permute-start | bytes 294920 | tf_op jit(solution)/shard_map/cond/branch_0_fun/ppermute | solution.py:88

commit v4 on v3

--- a/solution.py
+++ b/solution.py
@@ -115,7 +115,7 @@
 def choose_kernel(
     planes, entry_hbm, adapter_hbm, counts_hbm, tokens_ref, down_ref, up_ref, table_ref, *refs
 ):
-    others = planes - 2
+    others = planes - 1
     sends, tokens_out = refs[:others], refs[others : others + PLANE - 2]
     entry_ref, adapter_ref, counts_ref, small_sem, tokens_sem, sem = refs[others + PLANE - 2 :]
     me = lax.axis_index("wide")
@@ -165,35 +165,38 @@
     for d in reversed(range(planes)):
         held, place, count = listed(plane ^ d)
         most = jnp.maximum(most, count)
-        if d > 1:
-            for s in range(USUAL):
-                out = sends[d - 2].at[s]
+        if d > 0:
+            for s in range(sends[d - 1].shape[0]):
+                out = sends[d - 1].at[s]
                 for part, (ref, at) in enumerate(
                     ((down_ref, pl.ds(0, run)), (up_ref, pl.ds(run, up_run)))
                 ):
                     copies.append(
-                        pltpu.make_async_copy(ref.at[held[s]], out.at[:, at], sem.at[d - 2, s, part])
+                        pltpu.make_async_copy(ref.at[held[s]], out.at[:, at], sem.at[d - 1, s, part])
                     )
                     copies[-1].start()
         else:
             for s in range(SLOTS):
-                table_ref[PLANE + d * SLOTS + s] = held[s]
+                table_ref[PLANE + s] = held[s]
     for k in range(PLANE):
         i = column ^ k
         table_ref[k] = pick(jnp.where(plane % 2 == 0, i, PLANE - 1 - i), place)
-    table_ref[PLANE + 2 * SLOTS] = jnp.where(most > USUAL, 1, 0)
+    table_ref[PLANE + SLOTS] = jnp.where(most > USUAL, 1, 0)
     for copy in copies:
         copy.wait()
 
 
 def choose(planes, tokens, down, up, entry, adapter, counts):
     hbm = pl.BlockSpec(memory_space=pltpu.HBM)
-    others = planes - 2
-    send = jax.ShapeDtypeStruct((USUAL, 2, down.shape[2] + up.shape[2], down.shape[3]), down.dtype)
+    others = planes - 1
+    rows = (2, down.shape[2] + up.shape[2], down.shape[3])
+    sends = [
+        jax.ShapeDtypeStruct((SLOTS if d == 1 else USUAL,) + rows, down.dtype) for d in range(1, planes)
+    ]
     return pl.pallas_call(
         lambda *refs: choose_kernel(planes, *refs),
-        out_shape=[jax.ShapeDtypeStruct((PLANE + 2 * SLOTS + 1,), jnp.int32)]
-        + [send] * others
+        out_shape=[jax.ShapeDtypeStruct((PLANE + SLOTS + 1,), jnp.int32)]
+        + sends
         + [jax.ShapeDtypeStruct((2 * planes, BLK, down.shape[2]), tokens.dtype)] * (PLANE - 2),
         in_specs=[hbm] * 6,
         out_specs=[pl.BlockSpec(memory_space=pltpu.SMEM)]
@@ -204,33 +207,27 @@
             pltpu.SMEM(counts.shape, jnp.int32),
             pltpu.SemaphoreType.DMA((3,)),
             pltpu.SemaphoreType.DMA((PLANE - 2, 2 * planes)),
-            pltpu.SemaphoreType.DMA((others, USUAL, 2)),
+            pltpu.SemaphoreType.DMA((others, SLOTS, 2)),
         ],
         compiler_params=pltpu.CompilerParams(vmem_limit_bytes=57 * 2**20),
         name="choose",
     )(entry, adapter, counts, tokens, down, up)
 
 
-def gather_kernel(planes, table_ref, tokens_ref, down_ref, up_ref, own_ref, near_ref, pair_ref, tokens_sem, sem):
+def gather_kernel(planes, table_ref, tokens_ref, down_ref, up_ref, own_ref, pair_ref, tokens_sem, sem):
     column = lax.rem(lax.axis_index("wide"), PLANE)
     run, up_run = down_ref.shape[2], up_ref.shape[2]
     copies = []
     for core in range(2):
         at = lax.div(column, 2) * 2 + core
         copies += slices(tokens_ref, at, run, pair_ref.at[core], tokens_sem.at[core])
-    for d, out in enumerate((own_ref, near_ref)):
-        for s in range(out.shape[0]):
-            slot = table_ref[PLANE + d * SLOTS + s]
-            copies.append(
-                pltpu.make_async_copy(
-                    down_ref.at[slot], out.at[s, :, pl.ds(0, run)], sem.at[d, s, 0]
-                )
-            )
-            copies.append(
-                pltpu.make_async_copy(
-                    up_ref.at[slot], out.at[s, :, pl.ds(run, up_run)], sem.at[d, s, 1]
-                )
-            )
+    for s in range(SLOTS):
+        slot = table_ref[PLANE + s]
+        out = own_ref.at[s]
+        for part, (ref, rows) in enumerate(
+            ((down_ref, pl.ds(0, run)), (up_ref, pl.ds(run, up_run)))
+        ):
+            copies.append(pltpu.make_async_copy(ref.at[slot], out.at[:, rows], sem.at[s, part]))
     for copy in copies:
         copy.start()
     for copy in copies:
@@ -245,14 +242,13 @@
         lambda *refs: gather_kernel(planes, *refs),
         out_shape=[
             jax.ShapeDtypeStruct((SLOTS,) + rows, down.dtype),
-            jax.ShapeDtypeStruct((USUAL,) + rows, down.dtype),
         ]
         + [jax.ShapeDtypeStruct((2, 2 * planes, BLK, run), tokens.dtype)],
         in_specs=[pl.BlockSpec(memory_space=pltpu.SMEM)] + [hbm] * 3,
-        out_specs=[pl.BlockSpec(memory_space=pltpu.VMEM)] * 3,
+        out_specs=[pl.BlockSpec(memory_space=pltpu.VMEM)] * 2,
         scratch_shapes=[
             pltpu.SemaphoreType.DMA((2, 2 * planes)),
-            pltpu.SemaphoreType.DMA((2, SLOTS, 2)),
+            pltpu.SemaphoreType.DMA((SLOTS, 2)),
         ],
         compiler_params=pltpu.CompilerParams(vmem_limit_bytes=57 * 2**20),
         cost_estimate=pl.CostEstimate(flops=10**10, bytes_accessed=0, transcendentals=0),
@@ -304,7 +300,7 @@
 
         if flag:
             *outs, flag_ref = outs
-            flag_ref[0] = places_ref[PLANE + 2 * SLOTS]
+            flag_ref[0] = places_ref[PLANE + SLOTS]
         every = range(len(blocks))
         mine = sums_of(every, far) if far else {}
         here = [i for i in every if blocks[i] in near]
@@ -403,13 +399,12 @@
         adapter_of_request,
         token_blocks_per_request,
     )
-    far, across = sends[: planes - 2], sends[planes - 2 :]
-    own_factors, near, pair = gather(planes, places, tokens, adapter_down_weight, adapter_up_weight)
-    sends = sends + [near, pair]
+    factors, across = sends[: planes - 1], sends[planes - 1 :]
+    own_factors, pair = gather(planes, places, tokens, adapter_down_weight, adapter_up_weight)
+    sends = sends + [pair]
     run, up_run = adapter_down_weight.shape[2], adapter_up_weight.shape[2]
     whole, blocks = tuple(range(planes)), tuple(range(PLANE))
-    far = [swap(far[d - 2], d * PLANE) for d in range(2, planes)]
-    factors = [own_factors, swap(near, PLANE)] + far
+    factors = [own_factors] + [swap(factors[d - 1], d * PLANE) for d in whole[1:]]
     rows = [swap_cores(pair)] + [swap(across[k - 2], k) for k in range(2, PLANE)]
     *held, many = shrink(
         planes, SLOTS, run, (0, 1), (0, 1), (), places, rows[:1], factors[:1], flops=None, flag=True
@@ -426,10 +421,8 @@
         return finish(sums)
 
     def more(places, factors, rows, held, kept):
-        third = swap(jnp.concatenate([factors[d ^ 1][:1] for d in whole[1:]]), PLANE)
-        factors = [factors[0]] + [
-            jnp.concatenate([factors[d], third[d - 1 : d]]) for d in whole[1:]
-        ]
+        third = [swap(factors[d ^ 1][:1], PLANE) for d in whole[2:]]
+        factors = factors[:2] + [jnp.concatenate([factors[d], third[d - 2]]) for d in whole[2:]]
         sums = shrink(
             planes, SLOTS, run, blocks, (2, 3), whole[1:], places, rows, factors, held, whole, kept=kept
         )

time: 42.8 us -> 42.8 us (level)
    ppermute x8, waiting for transfers between devices: 18.7 us -> 18.3 us  [swap(): return lax.ppermute(value, 'wide', [(i, i ^ step) for i in range(count)])]
  transfers between devices with their start and end apart: 8 -> 8, of which waited for: 4 -> 5; matrix products, arithmetic and copies ran while one was open for 0% -> 0% of each run, Pallas kernels for 8% -> 8%
where the time goes in v4:
time: 42.8 us; the launch traced here: 42.6 us
  waiting for transfers between devices  18.3 us (43%)
  starting transfers between devices  9.49 us (22%)
  Pallas kernels  8.8 us (21%)
  blocking collectives  4.72 us (11%)
  between operations  1.31 us (3%)
    ppermute x8, waiting for transfers between devices, swap(): return lax.ppermute(value, 'wide', [(i, i ^ step) for i in range(count)])  18.3 us
    ppermute x8, starting transfers between devices, swap(): return lax.ppermute(value, 'wide', [(i, i ^ step) for i in range(count)])  9.49 us
    all_to_all x1, blocking collectives, swap_cores(): lax.all_to_all(value, 'wide', 0, 0, axis_index_groups=pairs, tiled=True)  4.72 us
    pallas_call x1, Pallas kernels, choose(): pl.pallas_call(lambda *refs: choose_kernel(planes, *refs), out_shape=[jax...  3.28 us
    pallas_call x2, Pallas kernels, shrink(): pl.pallas_call(kernel, out_shape=[jax.ShapeDtypeStruct((height, ranks), j...  2.26 us
    pallas_call x1, Pallas kernels, gather(): pl.pallas_call(lambda *refs: gather_kernel(planes, *refs), out_shape=[jax...  2.17 us
    pallas_call x1, Pallas kernels, expand(): pl.pallas_call(kernel, out_shape=[jax.ShapeDtypeStruct((BLK, columns), jn...  1.1 us
  transfers between devices with their start and end apart: 8, of which 5 were waited for; matrix products, arithmetic and copies ran while one was open for 0% of the time, Pallas kernels for 8%

profile of v4, /device:TPU:0, one launch (start us, length us, event | category | flops | bytes accessed | tf_op | source)
XLA Modules:
  0.0 42.6 jit_solution(1919939761380795722)
XLA Ops:
  0.6 3.3 %choose.1 = (s32[8]{0:T(128)S(1)}, bf16[3,2,288,128]{3,2,1,0:T(8,128)(2,1)S(1)}, bf16[2,2,288,128]{3,2,1,0:T(8,128)(2,1)S(1)}, bf16[2,2,288,128]{3,2,1,0:T(8,128...) custom-call(s32[16]{0:T(128)} %refs_0_.1, s32[4]{0:T(128)} %refs_1_.2, s32[4]{0:T(128)} %refs_2_.2, ...), custom_call_target="tpu_custom_call" | custom-call | tf_op jit(solution)/shard_map/choose/pallas_call | solution.py:196
  3.9 3.9 %collective-permute-start.11 = (bf16[2,2,288,128]{3,2,1,0:T(8,128)(2,1)S(1)}, bf16[2,2,288,128]{3,2,1,0:T(8,128)(2,1)S(1)}, u32[]{:S(2)}, u32[]{:S(2)}) collective-permute-start(bf16[2,2,288,128]{3,2,1,0:T(8,128)(2,1)S(1)} %get-tuple-element.106), channel_id=1, source_target_pairs={{0,8},{1,9},{2,10},{3,11},{4,12},{5,13},{6,14},{7,15},{8,0},{9,1},... | collective-permute-start | bytes 884744 | tf_op jit(solution)/shard_map/ppermute | solution.py:88
  7.9 1.3 %collective-permute-start.12 = (bf16[2,2,288,128]{3,2,1,0:T(8,128)(2,1)S(1)}, bf16[2,2,288,128]{3,2,1,0:T(8,128)(2,1)S(1)}, u32[]{:S(2)}, u32[]{:S(2)}) collective-permute-start(bf16[2,2,288,128]{3,2,1,0:T(8,128)(2,1)S(1)} %get-tuple-element.107), channel_id=1, source_target_pairs={{0,12},{1,13},{2,14},{3,15},{4,8},{5,9},{6,10},{7,11},{8,4},{9,5},... | collective-permute-start | bytes 884744 | tf_op jit(solution)/shard_map/ppermute | solution.py:88
  9.2 0.3 collective-permute-start.10
  9.5 1.5 %collective-permute-start.8 = (bf16[8,128,256]{2,1,0:T(8,128)(2,1)S(1)}, bf16[8,128,256]{2,1,0:T(8,128)(2,1)S(1)}, u32[]{:S(2)}, u32[]{:S(2)}) collective-permute-start(bf16[8,128,256]{2,1,0:T(8,128)(2,1)S(1)} %get-tuple-element.103), channel_id=1, source_target_pairs={{0,2},{1,3},{2,0},{3,1},{4,6},{5,7},{6,4},{7,5},{8,10},{9,11},{10,... | collective-permute-start | bytes 1572872 | tf_op jit(solution)/shard_map/ppermute | solution.py:88
  11.0 0.0 collective-permute-start.9
  11.0 2.2 %gather.1 = (bf16[3,2,288,128]{3,2,1,0:T(8,128)(2,1)S(1)}, bf16[2,8,128,256]{3,2,1,0:T(8,128)(2,1)S(1)}) custom-call(s32[8]{0:T(128)S(1)} %get-tuple-element.99.refs_0_.places_ref, bf16[128,8192]{1,0:T(8,128)(2,1)} %refs_1_.3, bf16[16,2,256,128]{3,2,1,0:T(8,128)(2,1)} %refs_2_.3, bf16[16,2,32,128]{3,2,1,0:T(8,128)(2,1)} %refs_3_.3), custom_call_target="tpu_custom_call" | custom-call | flops 10000000000 | tf_op jit(solution)/shard_map/gather/pallas_call | solution.py:241
  13.2 4.7 %all_to_all.5.refs_0_ = bf16[2,8,128,256]{3,2,1,0:T(8,128)(2,1)S(1)} all-to-all(bf16[2,8,128,256]{3,2,1,0:T(8,128)(2,1)S(1)} %get-tuple-element.100), channel_id=1, replica_groups={{0,1},{2,3},{4,5},{6,7},{8,9},{10,11},{12,13},{14,15},{16,17},{18,19},{..., dimensions={0} | all-to-all | bytes 2097152 | tf_op jit(solution)/shard_map/all_to_all | solution.py:94
  17.9 1.1 %shrink.5 = (f32[128,128]{1,0:T(8,128)S(1)}, f32[128,128]{1,0:T(8,128)S(1)}, s32[1]{0:T(128)}) custom-call(s32[8]{0:T(128)S(1)} %get-tuple-element.99.refs_0_.places_ref, bf16[2,8,128,256]{3,2,1,0:T(8,128)(2,1)S(1)} %all_to_all.5.refs_0_, bf16[3,2,288,128]{3,2,1,0:T(8,128)(2,1)S(1)} %get-tuple-element.101.refs_1_), custom_call_target="tpu_custom_call" | custom-call | tf_op jit(solution)/shard_map/shrink/pallas_call | solution.py:321
  19.7 8.7 %collective-permute-done.11 = bf16[2,2,288,128]{3,2,1,0:T(8,128)(2,1)S(1)} collective-permute-done((bf16[2,2,288,128]{3,2,1,0:T(8,128)(2,1)S(1)}, bf16[2,2,288,128]{3,2,1,0:T(8,128)(2,1)S(1)}, u32[]{:S(2)}, u32[]{:S(2)}) %collective-permute-start.11) | collective-permute-done | bytes 294944 | tf_op jit(solution)/shard_map/ppermute | solution.py:88
  28.4 0.0 collective-permute-done.12
  28.4 3.7 %collective-permute-done.10 = bf16[3,2,288,128]{3,2,1,0:T(8,128)(2,1)S(1)} collective-permute-done((bf16[3,2,288,128]{3,2,1,0:T(8,128)(2,1)S(1)}, bf16[3,2,288,128]{3,2,1,0:T(8,128)(2,1)S(1)}, u32[]{:S(2)}, u32[]{:S(2)}) %collective-permute-start.10) | collective-permute-done | bytes 442400 | tf_op jit(solution)/shard_map/ppermute | solution.py:88
  32.1 0.0 collective-permute-done.8
  32.1 0.8 %collective-permute-done.9 = bf16[8,128,256]{2,1,0:T(8,128)(2,1)S(1)} collective-permute-done((bf16[8,128,256]{2,1,0:T(8,128)(2,1)S(1)}, bf16[8,128,256]{2,1,0:T(8,128)(2,1)S(1)}, u32[]{:S(2)}, u32[]{:S(2)}) %collective-permute-start.9) | collective-permute-done | bytes 524320 | tf_op jit(solution)/shard_map/ppermute | solution.py:88
  32.9 9.7 %conditional.1 = ((bf16[128,1024]{1,0:T(8,128)(2,1)}, bf16[128,1024]{1,0:T(8,128)(2,1)})) conditional(s32[]{:T(128)} %bitcast, (s32[8]{0:T(128)S(1)}, bf16[2,8,128,256]{3,2,1,0:T(8,128)(2,1)S(1)}, bf16[8,128,256]{2,1,0:T(8,128)(2,1)S(1)}, bf16[8,128,256]{2,1,0:T(8,128)(2,1)S(1)}, bf16[3,2,288,128]{3,2,1,0:T(8,128)(2,1)S(1)}, ...), branch_computations={%region_0.0_spmd, %region_1.0_spmd} | conditional | flops 442368 | bytes 4718800 | solution.py:431
  32.9 1.2 %shrink.3 = (f32[384,128]{1,0:T(8,128)S(1)}, bf16[384,128]{1,0:T(8,128)(2,1)S(1)}, bf16[384,128]{1,0:T(8,128)(2,1)S(1)}, bf16[384,128]{1,0:T(8,128)(2,1)S(1)}) custom-call(s32[8]{0:T(128)S(1)} %get-tuple-element.52.places_ref, bf16[2,8,128,256]{3,2,1,0:T(8,128)(2,1)S(1)} %get-tuple-element.53.refs_0_, bf16[8,128,256]{2,1,0:T(8,128)(2,1)S(1)} %get-tuple-element.54.refs_1_, ...), custom_call_target="tpu_custom_call" | custom-call | tf_op jit(solution)/shard_map/cond/branch_0_fun/shrink/pallas_call | solution.py:321
  34.1 0.9 %collective-permute-start = (bf16[384,128]{1,0:T(8,128)(2,1)S(1)}, bf16[384,128]{1,0:T(8,128)(2,1)S(1)}, u32[]{:S(2)}, u32[]{:S(2)}) collective-permute-start(bf16[384,128]{1,0:T(8,128)(2,1)S(1)} %get-tuple-element.63), channel_id=1, source_target_pairs={{0,1},{1,0},{2,3},{3,2},{4,5},{5,4},{6,7},{7,6},{8,9},{9,8},{10,11... | collective-permute-start | bytes 294920 | tf_op jit(solution)/shard_map/cond/branch_0_fun/ppermute | solution.py:88
  35.0 1.5 %collective-permute-start.1 = (bf16[384,128]{1,0:T(8,128)(2,1)S(1)}, bf16[384,128]{1,0:T(8,128)(2,1)S(1)}, u32[]{:S(2)}, u32[]{:S(2)}) collective-permute-start(bf16[384,128]{1,0:T(8,128)(2,1)S(1)} %get-tuple-element.64), channel_id=1, source_target_pairs={{0,2},{1,3},{2,0},{3,1},{4,6},{5,7},{6,4},{7,5},{8,10},{9,11},{10,... | collective-permute-start | bytes 294920 | tf_op jit(solution)/shard_map/cond/branch_0_fun/ppermute | solution.py:88
  36.5 0.0 collective-permute-start.2
  36.5 0.0 collective-permute-done.refs_1_
  36.5 3.6 %collective-permute-done.1.refs_2_ = bf16[384,128]{1,0:T(8,128)(2,1)S(1)} collective-permute-done((bf16[384,128]{1,0:T(8,128)(2,1)S(1)}, bf16[384,128]{1,0:T(8,128)(2,1)S(1)}, u32[]{:S(2)}, u32[]{:S(2)}) %collective-permute-start.1) | collective-permute-done | bytes 98336 | tf_op jit(solution)/shard_map/cond/branch_0_fun/ppermute | solution.py:88
  40.1 1.5 %collective-permute-done.2.refs_3_ = bf16[384,128]{1,0:T(8,128)(2,1)S(1)} collective-permute-done((bf16[384,128]{1,0:T(8,128)(2,1)S(1)}, bf16[384,128]{1,0:T(8,128)(2,1)S(1)}, u32[]{:S(2)}, u32[]{:S(2)}) %collective-permute-start.2) | collective-permute-done | bytes 98336 | tf_op jit(solution)/shard_map/cond/branch_0_fun/ppermute | solution.py:88
  41.5 1.1 %expand.2 = (bf16[128,1024]{1,0:T(8,128)(2,1)}, bf16[128,1024]{1,0:T(8,128)(2,1)}) custom-call(f32[384,128]{1,0:T(8,128)S(1)} %get-tuple-element.62.refs_0_, bf16[384,128]{1,0:T(8,128)(2,1)S(1)} %collective-permute-done.refs_1_, bf16[384,128]{1,0:T(8,128)(2,1)S(1)} %collective-permute-done.1.refs_2_, bf16[384,128]{1,0:T(8,128)(2,1)S(1)} %collective-permute-done.2.refs_3_), custom_call_target="tpu_custom_call" | custom-call | tf_op jit(solution)/shard_map/cond/branch_0_fun/expand/pallas_call | solution.py:373
Async XLA Ops:
  3.9 24.5 %collective-permute-start.11 = (bf16[2,2,288,128]{3,2,1,0:T(8,128)(2,1)S(1)}, bf16[2,2,288,128]{3,2,1,0:T(8,128)(2,1)S(1)}, u32[]{:S(2)}, u32[]{:S(2)}) collective-permute-start(bf16[2,2,288,128]{3,2,1,0:T(8,128)(2,1)S(1)} %get-tuple-element.106), channel_id=1, source_target_pairs={{0,8},{1,9},{2,10},{3,11},{4,12},{5,13},{6,14},{7,15},{8,0},{9,1},... | collective-permute-start | bytes 884744 | tf_op jit(solution)/shard_map/ppermute | solution.py:88
  7.9 20.5 %collective-permute-start.12 = (bf16[2,2,288,128]{3,2,1,0:T(8,128)(2,1)S(1)}, bf16[2,2,288,128]{3,2,1,0:T(8,128)(2,1)S(1)}, u32[]{:S(2)}, u32[]{:S(2)}) collective-permute-start(bf16[2,2,288,128]{3,2,1,0:T(8,128)(2,1)S(1)} %get-tuple-element.107), channel_id=1, source_target_pairs={{0,12},{1,13},{2,14},{3,15},{4,8},{5,9},{6,10},{7,11},{8,4},{9,5},... | collective-permute-start | bytes 884744 | tf_op jit(solution)/shard_map/ppermute | solution.py:88
  9.2 22.9 %collective-permute-start.10 = (bf16[3,2,288,128]{3,2,1,0:T(8,128)(2,1)S(1)}, bf16[3,2,288,128]{3,2,1,0:T(8,128)(2,1)S(1)}, u32[]{:S(2)}, u32[]{:S(2)}) collective-permute-start(bf16[3,2,288,128]{3,2,1,0:T(8,128)(2,1)S(1)} %get-tuple-element.105), channel_id=1, source_target_pairs={{0,4},{1,5},{2,6},{3,7},{4,0},{5,1},{6,2},{7,3},{8,12},{9,13},{10,... | collective-permute-start | bytes 1327112 | tf_op jit(solution)/shard_map/ppermute | solution.py:88
  9.5 22.6 %collective-permute-start.8 = (bf16[8,128,256]{2,1,0:T(8,128)(2,1)S(1)}, bf16[8,128,256]{2,1,0:T(8,128)(2,1)S(1)}, u32[]{:S(2)}, u32[]{:S(2)}) collective-permute-start(bf16[8,128,256]{2,1,0:T(8,128)(2,1)S(1)} %get-tuple-element.103), channel_id=1, source_target_pairs={{0,2},{1,3},{2,0},{3,1},{4,6},{5,7},{6,4},{7,5},{8,10},{9,11},{10,... | collective-permute-start | bytes 1572872 | tf_op jit(solution)/shard_map/ppermute | solution.py:88
  11.0 21.9 %collective-permute-start.9 = (bf16[8,128,256]{2,1,0:T(8,128)(2,1)S(1)}, bf16[8,128,256]{2,1,0:T(8,128)(2,1)S(1)}, u32[]{:S(2)}, u32[]{:S(2)}) collective-permute-start(bf16[8,128,256]{2,1,0:T(8,128)(2,1)S(1)} %get-tuple-element.104), channel_id=1, source_target_pairs={{0,3},{1,2},{2,1},{3,0},{4,7},{5,6},{6,5},{7,4},{8,11},{9,10},{10,... | collective-permute-start | bytes 1572872 | tf_op jit(solution)/shard_map/ppermute | solution.py:88
  34.1 2.4 %collective-permute-start = (bf16[384,128]{1,0:T(8,128)(2,1)S(1)}, bf16[384,128]{1,0:T(8,128)(2,1)S(1)}, u32[]{:S(2)}, u32[]{:S(2)}) collective-permute-start(bf16[384,128]{1,0:T(8,128)(2,1)S(1)} %get-tuple-element.63), channel_id=1, source_target_pairs={{0,1},{1,0},{2,3},{3,2},{4,5},{5,4},{6,7},{7,6},{8,9},{9,8},{10,11... | collective-permute-start | bytes 294920 | tf_op jit(solution)/shard_map/cond/branch_0_fun/ppermute | solution.py:88
  35.0 5.1 %collective-permute-start.1 = (bf16[384,128]{1,0:T(8,128)(2,1)S(1)}, bf16[384,128]{1,0:T(8,128)(2,1)S(1)}, u32[]{:S(2)}, u32[]{:S(2)}) collective-permute-start(bf16[384,128]{1,0:T(8,128)(2,1)S(1)} %get-tuple-element.64), channel_id=1, source_target_pairs={{0,2},{1,3},{2,0},{3,1},{4,6},{5,7},{6,4},{7,5},{8,10},{9,11},{10,... | collective-permute-start | bytes 294920 | tf_op jit(solution)/shard_map/cond/branch_0_fun/ppermute | solution.py:88
  36.5 5.1 %collective-permute-start.2 = (bf16[384,128]{1,0:T(8,128)(2,1)S(1)}, bf16[384,128]{1,0:T(8,128)(2,1)S(1)}, u32[]{:S(2)}, u32[]{:S(2)}) collective-permute-start(bf16[384,128]{1,0:T(8,128)(2,1)S(1)} %get-tuple-element.65), channel_id=1, source_target_pairs={{0,3},{1,2},{2,1},{3,0},{4,7},{5,6},{6,5},{7,4},{8,11},{9,10},{10,... | collective-permute-start | bytes 294920 | tf_op jit(solution)/shard_map/cond/branch_0_fun/ppermute | solution.py:88
